TPU v7x, 32 devices: a whole 2x2x4 slice. The times are simulated.
32 devices in a mesh: ctx: 16 (over z, y, core), head: 2 (over x).
Axes of the slice: x: 2, y: 2, z: 4, core: 2. Of those that a mesh axis runs over, the one named last changes fastest.
Arguments:
- queries: bfloat16 [4096, 8192], P(('ctx', 'head')), may hold values from -200 to 200
- key_rows: bfloat16 [4096, 1024], P(('ctx', 'head')), may hold values from -6 to 6
- value_rows: bfloat16 [4096, 1024], P(('ctx', 'head')), may hold values from -6 to 6
- span_order: int32 [32], replicated, may hold values from 0 to 31, each once
Outputs:
- attended: bfloat16 [4096, 8192], P(('ctx', 'head'))
Inputs may be any that keep to these rules, and one draw needn't show every extreme that they name: Stored span j holds sequence positions span_order[j] * 128 to span_order[j] * 128 + 127; each number appears once.
All inputs are finite; a program needn't handle non-finite values.
Results may differ from a plain program's by a relative error of at most 0.005.
Values may be sent and summed in bfloat16 or wider, within the bound.
No kernel may reach another device: no remote copies, remote signals or barrier semaphores. Data moves between devices by JAX's collectives and lax.ppermute only.
A program may use at most 256 MiB of HBM per device.

v0:
```python
import functools
import math

import jax
import jax.numpy as jnp
from jax import lax
from jax.experimental import pallas as pl
from jax.experimental.pallas import tpu as pltpu
from jax.sharding import Mesh
from jax.sharding import PartitionSpec as P

HQ = 64
KVH = 8
HD = 128
SPAN = 128
GROUP = HQ // KVH
ROWS = GROUP * SPAN
SCALE = HD**-0.5 * math.log2(math.e)
EXTRA = 16
BLOCK = 4
NT = (((1,), (1,)), ((), ()))
GROUP_AXES = ("inner", "head")


def queries_of(q_ref):
    return jnp.concatenate([q_ref[:, g * HD : (g + 1) * HD] for g in range(GROUP)], 0)


def scores(keys, q_ref):
    return lax.dot_general(keys, queries_of(q_ref), NT, preferred_element_type=jnp.float32) * SCALE


def blend(values, weights):
    ones = jnp.ones((EXTRA, values.shape[1]), jnp.bfloat16)
    values = jnp.concatenate([values, ones], 0)
    return jnp.dot(values, weights.astype(jnp.bfloat16), preferred_element_type=jnp.float32)


def causal(s):
    key = lax.broadcasted_iota(jnp.int32, (SPAN, ROWS), 0)
    row = lax.broadcasted_iota(jnp.int32, (SPAN, ROWS), 1) % SPAN
    return jnp.where(key <= row, s, -1e30)


def gather(kv_ref, slots):
    return (
        jnp.concatenate([kv_ref[s, :SPAN] for s in slots], 0),
        jnp.concatenate([kv_ref[s, SPAN:] for s in slots], 1),
    )


def list_spans(order_ref, slot_ref, list_ref, rank_ref, wanted):
    spans = order_ref.shape[0]

    def invert(j, carry):
        slot_ref[order_ref[j]] = j
        return carry

    lax.fori_loop(0, spans, invert, 0)

    def take(t, count):
        j = slot_ref[t]
        rank_ref[t] = count
        list_ref[count] = j
        return count + jnp.where(wanted(j), 1, 0)

    lax.fori_loop(0, spans, take, jnp.int32(0))


def near_kernel(n_kv, *refs):
    where_ref, order_ref, q_ref = refs[:3]
    kv_refs = refs[3 : 3 + n_kv]
    acc_ref, m_ref, kv_ref, slot_ref, list_ref, rank_ref = refs[3 + n_kv :]
    step = pl.program_id(0)

    @pl.when(step == 0)
    def _():
        first = where_ref[1]
        last = first + where_ref[2]
        list_spans(order_ref, slot_ref, list_ref, rank_ref, lambda j: jnp.logical_or(j < first, j >= last))
        for index, piece_ref in enumerate(kv_refs):
            for j in range(piece_ref.shape[0]):
                kv_ref[where_ref[3 + index] + j] = piece_ref[j]

    rank = rank_ref[order_ref[where_ref[0] + step]]

    def first_block(count):
        keys, values = gather(kv_ref, [list_ref[rank + 1 - count + t] for t in range(count)])
        s = scores(keys, q_ref)
        own = causal(s[(count - 1) * SPAN :])
        s = jnp.concatenate([s[: (count - 1) * SPAN], own], 0) if count > 1 else own
        m = jnp.max(s, axis=0, keepdims=True)
        m_ref[0] = jnp.broadcast_to(m, m_ref.shape[1:])
        acc_ref[0] = blend(values, jnp.exp2(s - m))

    for count in range(1, BLOCK + 1):

        @pl.when(rank % BLOCK == count - 1)
        def _(count=count):
            first_block(count)

    def block(b, carry):
        keys, values = gather(kv_ref, [list_ref[b * BLOCK + t] for t in range(BLOCK)])
        acc_ref[0] += blend(values, jnp.exp2(scores(keys, q_ref) - m_ref[0, :1]))
        return carry

    lax.fori_loop(0, rank // BLOCK, block, 0)


def far_kernel(n_kv, n_far, *refs):
    where_ref, order_ref, q_ref, acc_in, m_in = refs[:5]
    kv_refs = refs[5 : 5 + n_kv]
    o_ref, acc_ref, run_ref, kv_ref, slot_ref, list_ref, rank_ref = refs[5 + n_kv :]
    step = pl.program_id(0)
    first = where_ref[1]
    last = first + where_ref[2]

    @pl.when(step == 0)
    def _():
        list_spans(order_ref, slot_ref, list_ref, rank_ref, lambda j: jnp.logical_and(j >= first, j < last))
        for index in range(n_kv - n_far, n_kv):

            @pl.when(where_ref[3 + index] >= 0)
            def _(piece_ref=kv_refs[index]):
                for j in range(piece_ref.shape[0]):
                    kv_ref[j] = piece_ref[j]

    p = order_ref[where_ref[0] + step]
    acc_ref[...] = acc_in[0]
    if n_far:
        count = rank_ref[p]

        def block(start, size):
            keys, values = gather(kv_ref, [list_ref[start + t] - first for t in range(size)])
            acc_ref[...] += blend(values, jnp.exp2(scores(keys, q_ref) - m_in[0, :1]))

        def whole(b, carry):
            block(b * BLOCK, BLOCK)
            return carry

        lax.fori_loop(0, count // BLOCK, whole, 0)
        for size in range(1, BLOCK):

            @pl.when(count % BLOCK == size)
            def _(size=size):
                block(count - size, size)

    @pl.when(jnp.logical_not(jnp.max(acc_ref[HD : HD + 8]) < 1e30))
    def _():
        run_ref[...] = jnp.full_like(run_ref, -1e30)
        acc_ref[...] = jnp.zeros_like(acc_ref)
        for index, piece_ref in enumerate(kv_refs):
            base = where_ref[3 + index]

            def careful(j, carry, piece_ref=piece_ref, base=base):
                other = order_ref[jnp.maximum(base, 0) + j]

                @pl.when(jnp.logical_and(base >= 0, other <= p))
                def _():
                    s = scores(piece_ref[j, :SPAN], q_ref)
                    s = jnp.where(other < p, s, causal(s))
                    old = run_ref[...]
                    new = jnp.maximum(old, jnp.max(s, axis=0, keepdims=True))
                    run_ref[...] = new
                    fresh = blend(piece_ref[j, SPAN:], jnp.exp2(s - new[:1]))
                    acc_ref[...] = acc_ref[...] * jnp.exp2(old - new)[:1] + fresh

                return carry

            lax.fori_loop(0, piece_ref.shape[0], careful, 0)

    result = acc_ref[:HD] * (1.0 / acc_ref[HD : HD + 1])
    for g in range(GROUP):
        o_ref[:, g * HD : (g + 1) * HD] = result[:, g * SPAN : (g + 1) * SPAN].T.astype(o_ref.dtype)


def attention(q, near, far, near_bases, far_bases, far_first, far_count, first_span, span_order):
    q_spans = q.shape[0] // SPAN
    spans = span_order.shape[0]
    where = jnp.stack([first_span, far_first, far_count, *near_bases, *far_bases]).astype(jnp.int32)
    q_spec = pl.BlockSpec((SPAN, GROUP * HD), lambda i, *_: (i, 0))
    acc_spec = pl.BlockSpec((1, HD + EXTRA, ROWS), lambda i, *_: (i, 0, 0))
    m_spec = pl.BlockSpec((1, 8, ROWS), lambda i, *_: (i, 0, 0))
    piece_specs = [pl.BlockSpec(piece.shape, lambda i, *_: (0, 0, 0)) for piece in near + far]
    lists = [pltpu.SMEM((spans,), jnp.int32)] * 3
    elements = q.shape[0] * GROUP * spans * SPAN // 2
    limit = pltpu.CompilerParams(vmem_limit_bytes=40 * 2**20)

    def cost(part):
        return pl.CostEstimate(
            flops=int(8 * HD * elements * part),
            bytes_accessed=4 * q.size + 4 * spans * SPAN * HD,
            transcendentals=int(elements * part),
        )

    acc, m = pl.pallas_call(
        functools.partial(near_kernel, len(near)),
        grid_spec=pltpu.PrefetchScalarGridSpec(
            num_scalar_prefetch=2,
            grid=(q_spans,),
            in_specs=[q_spec] + piece_specs[: len(near)],
            out_specs=[acc_spec, m_spec],
            scratch_shapes=[pltpu.VMEM((spans, SPAN + HD, SPAN), jnp.bfloat16), *lists],
        ),
        out_shape=[
            jax.ShapeDtypeStruct((q_spans, HD + EXTRA, ROWS), jnp.float32),
            jax.ShapeDtypeStruct((q_spans, 8, ROWS), jnp.float32),
        ],
        compiler_params=limit,
        cost_estimate=cost(0.75),
        name="near",
    )(where, span_order, q, *near)
    return pl.pallas_call(
        functools.partial(far_kernel, len(near) + len(far), len(far)),
        grid_spec=pltpu.PrefetchScalarGridSpec(
            num_scalar_prefetch=2,
            grid=(q_spans,),
            in_specs=[q_spec, acc_spec, m_spec] + piece_specs,
            out_specs=q_spec,
            scratch_shapes=[
                pltpu.VMEM((HD + EXTRA, ROWS), jnp.float32),
                pltpu.VMEM((8, ROWS), jnp.float32),
                pltpu.VMEM((near[0].shape[0], SPAN + HD, SPAN), jnp.bfloat16),
                *lists,
            ],
        ),
        out_shape=jax.ShapeDtypeStruct(q.shape, q.dtype),
        compiler_params=limit,
        cost_estimate=cost(0.25),
        name="far",
    )(where, span_order, q, acc, m, *near, *far)


def pack_kernel(k_ref, v_ref, o_ref):
    for h in range(KVH):
        o_ref[h, :SPAN] = k_ref[:, h * HD : (h + 1) * HD]
        o_ref[h, SPAN:] = v_ref[:, h * HD : (h + 1) * HD].T


def to_head_owners(key_rows, value_rows):
    rows = key_rows.shape[0]
    exchange = functools.partial(
        lax.all_to_all, axis_name=GROUP_AXES, split_axis=0, concat_axis=0, tiled=False
    )
    if rows == SPAN:
        packed = pl.pallas_call(
            pack_kernel, out_shape=jax.ShapeDtypeStruct((KVH, SPAN + HD, SPAN), key_rows.dtype), name="pack"
        )(key_rows, value_rows)
        return exchange(packed)
    packed = jnp.concatenate([key_rows.reshape(rows, KVH, HD), value_rows.reshape(rows, KVH, HD)], 2)
    own = exchange(packed.transpose(1, 0, 2)).reshape(KVH * rows // SPAN, SPAN, 2 * HD)
    return jnp.concatenate([own[:, :, :HD], own[:, :, HD:].transpose(0, 2, 1)], 1)


def shards(outer, queries, key_rows, value_rows, span_order):
    rows = queries.shape[0]
    place = lax.axis_index("outer")
    group_rows = KVH * rows
    group_spans = group_rows // SPAN
    own = to_head_owners(key_rows, value_rows)
    q = queries.reshape(rows, KVH, GROUP * HD).transpose(1, 0, 2)
    q = lax.all_to_all(q, GROUP_AXES, split_axis=0, concat_axis=0, tiled=False).reshape(group_rows, GROUP * HD)
    if outer == 4:
        up = lax.ppermute(own, "outer", [(i, (i + 1) % outer) for i in range(outer)])
        down = lax.ppermute(own, "outer", [(i, (i - 1) % outer) for i in range(outer)])
        far_up = lax.ppermute(up, "outer", [(1, 2), (2, 3)])
        far_down = lax.ppermute(down, "outer", [(1, 0), (2, 1)])
        near = [own, up, down]
        near_bases = [(place + step) % outer * group_spans for step in (0, outer - 1, 1)]
        far = [far_up, far_down]
        far_first = (place + 2) % outer * group_spans
        far_count = jnp.int32(group_spans)
        far_bases = [jnp.where(place >= 2, far_first, -1), jnp.where(place < 2, far_first, -1)]
    else:
        near = [lax.all_gather(own, "outer", axis=0, tiled=True)]
        near_bases = [jnp.int32(0)]
        far, far_bases, far_first, far_count = [], [], jnp.int32(0), jnp.int32(0)
    out = attention(q, near, far, near_bases, far_bases, far_first, far_count, place * group_spans, span_order)
    out = lax.all_to_all(out.reshape(KVH, rows, GROUP * HD), GROUP_AXES, split_axis=0, concat_axis=0, tiled=False)
    return out.transpose(1, 0, 2).reshape(rows, HQ * HD)


def solution(mesh):
    ctx, head = mesh.devices.shape
    inner = KVH // head
    split = Mesh(mesh.devices.reshape(ctx // inner, inner, head), ("outer", "inner", "head"))
    spec = P(("outer", "inner", "head"), None)
    return jax.shard_map(
        functools.partial(shards, ctx // inner),
        mesh=split,
        in_specs=(spec, spec, spec, P()),
        out_specs=spec,
        check_vma=False,
    )
```

profile of v0, /device:TPU:25, one launch (start us, length us, event | category | flops | bytes accessed | tf_op | source)
XLA Modules:
  0.0 117.2 jit_solution(12804317687360038518)
XLA Ops:
  0.0 0.0 copy-start.1
  0.0 2.1 %pack.1 = bf16[8,256,128]{2,1,0:T(8,128)(2,1)} custom-call(bf16[128,1024]{1,0:T(8,128)(2,1)} %k_ref.1, bf16[128,1024]{1,0:T(8,128)(2,1)} %v_ref.1), custom_call_target="tpu_custom_call" | custom-call | tf_op jit(solution)/shard_map/pack/pallas_call | solution.py:246
  2.1 4.4 %all-to-all-start.1 = ((bf16[8,256,128]{2,1,0:T(8,128)(2,1)}), bf16[8,256,128]{2,1,0:T(8,128)(2,1)S(1)}, u32[]{:S(2)}, u32[]{:S(2)}) async-start(bf16[8,256,128]{2,1,0:T(8,128)(2,1)} %pack.1), calls=%async_computation.1 | async-start | bytes 1048576 | tf_op jit(solution)/shard_map/all_to_all | solution.py:249
  6.5 0.0 copy-done.1
  6.5 1.5 %copy.10 = bf16[16,8,8,1024]{3,2,0,1:T(8,128)(2,1)} copy(bf16[16,8,8,1024]{3,2,1,0:T(8,128)(2,1)S(1)} %bitcast.24) | data formatting | bytes 4194304 | tf_op jit(solution)/shard_map/reshape | solution.py:261
  8.0 6.9 %all-to-all-done.1.refs_3_.refs_5_ = bf16[8,256,128]{2,1,0:T(8,128)(2,1)S(1)} async-done(((bf16[8,256,128]{2,1,0:T(8,128)(2,1)}), bf16[8,256,128]{2,1,0:T(8,128)(2,1)S(1)}, u32[]{:S(2)}, u32[]{:S(2)}) %all-to-all-start.1) | async-done | bytes 524320 | tf_op jit(solution)/shard_map/all_to_all | solution.py:249
  14.9 0.0 copy-start
  14.9 4.5 %all-to-all-start = ((bf16[8,128,1024]{2,1,0:T(8,128)(2,1)}), bf16[8,128,1024]{2,1,0:T(8,128)(2,1)S(1)}, u32[]{:S(2)}, u32[]{:S(2)}) async-start(bf16[8,128,1024]{2,1,0:T(8,128)(2,1)} %bitcast.22), calls=%async_computation | async-start | bytes 4194304 | tf_op jit(solution)/shard_map/all_to_all | solution.py:262
  19.4 0.2 collective-permute-start.1
  19.6 3.1 %collective-permute-start = (bf16[8,256,128]{2,1,0:T(8,128)(2,1)S(1)}, bf16[8,256,128]{2,1,0:T(8,128)(2,1)}, u32[]{:S(2)}, u32[]{:S(2)}) collective-permute-start(bf16[8,256,128]{2,1,0:T(8,128)(2,1)S(1)} %all-to-all-done.1.refs_3_.refs_5_), channel_id=1, source_target_pairs={{0,8},{8,16},{16,24},{24,0},{1,9},{9,17},{17,25},{25,1},{2,10},{10... | collective-permute-start | bytes 1572872 | tf_op jit(solution)/shard_map/ppermute | solution.py:264
  22.7 0.1 stack.31.refs_0_
  22.8 11.9 %collective-permute-done.1.refs_5_.refs_7_ = bf16[8,256,128]{2,1,0:T(8,128)(2,1)S(1)} collective-permute-done((bf16[8,256,128]{2,1,0:T(8,128)(2,1)S(1)}, bf16[8,256,128]{2,1,0:T(8,128)(2,1)S(1)}, u32[]{:S(2)}, u32[]{:S(2)}) %collective-permute-start.1) | collective-permute-done | bytes 524320 | tf_op jit(solution)/shard_map/ppermute | solution.py:265
  34.6 1.5 %collective-permute-start.3 = (bf16[8,256,128]{2,1,0:T(8,128)(2,1)S(1)}, bf16[8,256,128]{2,1,0:T(8,128)(2,1)}, u32[]{:S(2)}, u32[]{:S(2)}) collective-permute-start(bf16[8,256,128]{2,1,0:T(8,128)(2,1)S(1)} %collective-permute-done.1.refs_5_.refs_7_), channel_id=1, source_target_pairs={{8,0},{16,8},{9,1},{17,9},{10,2},{18,10},{11,3},{19,11},{12,4},{20... | collective-permute-start | bytes 1572872 | tf_op jit(solution)/shard_map/ppermute | solution.py:267
  36.1 7.9 %collective-permute-done.refs_4_.refs_6_ = bf16[8,256,128]{2,1,0:T(8,128)(2,1)} collective-permute-done((bf16[8,256,128]{2,1,0:T(8,128)(2,1)S(1)}, bf16[8,256,128]{2,1,0:T(8,128)(2,1)}, u32[]{:S(2)}, u32[]{:S(2)}) %collective-permute-start) | collective-permute-done | bytes 524320 | tf_op jit(solution)/shard_map/ppermute | solution.py:264
  44.0 1.3 %collective-permute-start.2 = (bf16[8,256,128]{2,1,0:T(8,128)(2,1)}, bf16[8,256,128]{2,1,0:T(8,128)(2,1)}, u32[]{:S(2)}, u32[]{:S(2)}) collective-permute-start(bf16[8,256,128]{2,1,0:T(8,128)(2,1)} %collective-permute-done.refs_4_.refs_6_), channel_id=1, source_target_pairs={{8,16},{16,24},{9,17},{17,25},{10,18},{18,26},{11,19},{19,27},{12,... | collective-permute-start | bytes 1572872 | tf_op jit(solution)/shard_map/ppermute | solution.py:266
  45.3 0.0 all-to-all-done
  45.3 0.0 copy-done
  45.3 27.3 %near.1 = (f32[8,144,1024]{2,1,0:T(8,128)S(1)}, f32[8,8,1024]{2,1,0:T(8,128)S(1)}) custom-call(s32[8]{0:T(128)S(1)} %stack.31.refs_0_, s32[32]{0:T(128)S(1)} %copy-done, bf16[1024,1024]{1,0:T(8,128)(2,1)S(1)} %bitcast.19, bf16[8,256,128]{2,1,0:T(8,128)(2,1)S(1)} %all-to-all-done.1.refs_3_.refs_5_, bf16[8,256,128]{2,1,0:T(8,128)(2,1)} %collective-permute-done.refs_4_.refs_6_, ...), custom_call_target="tpu_custom_call" | custom-call | flops 12884901888 | bytes 6291456 | tf_op jit(solution)/shard_map/near/pallas_call | solution.py:196
  72.6 0.0 collective-permute-done.3.refs_9_
  72.6 0.0 collective-permute-done.2.refs_8_
  72.6 12.4 %far.1 = bf16[1024,1024]{1,0:T(8,128)(2,1)S(1)} custom-call(s32[8]{0:T(128)S(1)} %stack.31.refs_0_, s32[32]{0:T(128)S(1)} %copy-done, bf16[1024,1024]{1,0:T(8,128)(2,1)S(1)} %bitcast.20, f32[8,144,1024]{2,1,0:T(8,128)S(1)} %get-tuple-element.7.refs_3_, f32[8,8,1024]{2,1,0:T(8,128)S(1)} %get-tuple-element.8.refs_4_, ...), custom_call_target="tpu_custom_call" | custom-call | flops 4294967296 | bytes 6291456 | tf_op jit(solution)/shard_map/far/pallas_call | solution.py:213
  85.0 30.7 %all_to_all.15 = bf16[8,128,1024]{2,1,0:T(8,128)(2,1)S(1)} all-to-all(bf16[8,128,1024]{2,1,0:T(8,128)(2,1)S(1)} %bitcast.21), channel_id=1, replica_groups=mesh['outer'=4,'inner'=4,'head'=2] {'inner','head'}, dimensions={0} | all-to-all | bytes 4194304 | tf_op jit(solution)/shard_map/all_to_all | solution.py:279
  115.6 1.5 %copy.8 = bf16[8,16,8,1024]{3,2,0,1:T(8,128)(2,1)} copy(bf16[8,16,8,1024]{3,2,1,0:T(8,128)(2,1)S(1)} %bitcast.23) | data formatting | bytes 4194304 | tf_op jit(solution)/shard_map/reshape | solution.py:280
Async XLA Ops:
  0.0 6.5 %copy-start.1 = (bf16[128,8192]{1,0:T(8,128)(2,1)S(1)}, bf16[128,8192]{1,0:T(8,128)(2,1)}, u32[]{:S(2)}) copy-start(bf16[128,8192]{1,0:T(8,128)(2,1)} %param.4) | copy-start | bytes 6291460
  2.1 12.8 %all-to-all-start.1 = ((bf16[8,256,128]{2,1,0:T(8,128)(2,1)}), bf16[8,256,128]{2,1,0:T(8,128)(2,1)S(1)}, u32[]{:S(2)}, u32[]{:S(2)}) async-start(bf16[8,256,128]{2,1,0:T(8,128)(2,1)} %pack.1), calls=%async_computation.1 | async-start | bytes 1048576 | tf_op jit(solution)/shard_map/all_to_all | solution.py:249
  14.9 30.3 %copy-start = (s32[32]{0:T(128)S(1)}, s32[32]{0:T(128)}, u32[]{:S(2)}) copy-start(s32[32]{0:T(128)} %refs_1_.3) | copy-start | bytes 388
  14.9 30.3 %all-to-all-start = ((bf16[8,128,1024]{2,1,0:T(8,128)(2,1)}), bf16[8,128,1024]{2,1,0:T(8,128)(2,1)S(1)}, u32[]{:S(2)}, u32[]{:S(2)}) async-start(bf16[8,128,1024]{2,1,0:T(8,128)(2,1)} %bitcast.22), calls=%async_computation | async-start | bytes 4194304 | tf_op jit(solution)/shard_map/all_to_all | solution.py:262
  19.4 15.2 %collective-permute-start.1 = (bf16[8,256,128]{2,1,0:T(8,128)(2,1)S(1)}, bf16[8,256,128]{2,1,0:T(8,128)(2,1)S(1)}, u32[]{:S(2)}, u32[]{:S(2)}) collective-permute-start(bf16[8,256,128]{2,1,0:T(8,128)(2,1)S(1)} %all-to-all-done.1.refs_3_.refs_5_), channel_id=1, source_target_pairs={{0,24},{8,0},{16,8},{24,16},{1,25},{9,1},{17,9},{25,17},{2,26},{10... | collective-permute-start | bytes 1572872 | tf_op jit(solution)/shard_map/ppermute | solution.py:265
  19.6 24.4 %collective-permute-start = (bf16[8,256,128]{2,1,0:T(8,128)(2,1)S(1)}, bf16[8,256,128]{2,1,0:T(8,128)(2,1)}, u32[]{:S(2)}, u32[]{:S(2)}) collective-permute-start(bf16[8,256,128]{2,1,0:T(8,128)(2,1)S(1)} %all-to-all-done.1.refs_3_.refs_5_), channel_id=1, source_target_pairs={{0,8},{8,16},{16,24},{24,0},{1,9},{9,17},{17,25},{25,1},{2,10},{10... | collective-permute-start | bytes 1572872 | tf_op jit(solution)/shard_map/ppermute | solution.py:264
  34.6 37.9 %collective-permute-start.3 = (bf16[8,256,128]{2,1,0:T(8,128)(2,1)S(1)}, bf16[8,256,128]{2,1,0:T(8,128)(2,1)}, u32[]{:S(2)}, u32[]{:S(2)}) collective-permute-start(bf16[8,256,128]{2,1,0:T(8,128)(2,1)S(1)} %collective-permute-done.1.refs_5_.refs_7_), channel_id=1, source_target_pairs={{8,0},{16,8},{9,1},{17,9},{10,2},{18,10},{11,3},{19,11},{12,4},{20... | collective-permute-start | bytes 1572872 | tf_op jit(solution)/shard_map/ppermute | solution.py:267
  44.0 28.6 %collective-permute-start.2 = (bf16[8,256,128]{2,1,0:T(8,128)(2,1)}, bf16[8,256,128]{2,1,0:T(8,128)(2,1)}, u32[]{:S(2)}, u32[]{:S(2)}) collective-permute-start(bf16[8,256,128]{2,1,0:T(8,128)(2,1)} %collective-permute-done.refs_4_.refs_6_), channel_id=1, source_target_pairs={{8,16},{16,24},{9,17},{17,25},{10,18},{18,26},{11,19},{19,27},{12,... | collective-permute-start | bytes 1572872 | tf_op jit(solution)/shard_map/ppermute | solution.py:266
where the time goes:
time: 117 us
  Pallas kernels  41.7 us (36%)
  blocking collectives  30.7 us (26%)
  waiting for transfers between devices  26.6 us (23%)
  starting transfers between devices  14.9 us (13%)
  local copies, waits for them, and re-layouts  3.15 us (3%)
    all_to_all x1, blocking collectives, shards(): lax.all_to_all(out.reshape(KVH, rows, GROUP * HD), GROUP_AXES, split_axis...  30.7 us
    pallas_call x1, Pallas kernels, attention(): pl.pallas_call(functools.partial(near_kernel, len(near)), grid_spec=pltpu...  27.3 us
    pallas_call x1, Pallas kernels, attention(): pl.pallas_call(functools.partial(far_kernel, len(near) + len(far), len(fa...  12.4 us
    ppermute x1, waiting for transfers between devices, shards(): lax.ppermute(own, 'outer', [(i, (i - 1) % outer) for i in range(outer)])  11.9 us
    ppermute x1, waiting for transfers between devices, shards(): lax.ppermute(own, 'outer', [(i, (i + 1) % outer) for i in range(outer)])  7.85 us
    all_to_all x1, waiting for transfers between devices, to_head_owners(): return exchange(packed)  6.92 us
    all_to_all x1, starting transfers between devices, shards(): lax.all_to_all(q, GROUP_AXES, split_axis=0, concat_axis=0, tiled=False)  4.46 us
    all_to_all x1, starting transfers between devices, to_head_owners(): return exchange(packed)  4.39 us
  transfers between devices with their start and end apart: 6, of which 3 were waited for; matrix products, arithmetic and copies ran while one was open for 1% of the time, Pallas kernels for 23%

commit v1 on v0

--- a/solution.py
+++ b/solution.py
@@ -20,6 +20,7 @@
 BLOCK = 4
 NT = (((1,), (1,)), ((), ()))
 GROUP_AXES = ("inner", "head")
+PARTS = ((5, 7, 1, 4), (3, 6, 2, 0))
 
 
 def queries_of(q_ref):
@@ -107,10 +108,11 @@
     lax.fori_loop(0, rank // BLOCK, block, 0)
 
 
-def far_kernel(n_kv, n_far, *refs):
-    where_ref, order_ref, q_ref, acc_in, m_in = refs[:5]
-    kv_refs = refs[5 : 5 + n_kv]
-    o_ref, acc_ref, run_ref, kv_ref, slot_ref, list_ref, rank_ref = refs[5 + n_kv :]
+def far_kernel(n_kv, n_far, n_out, *refs):
+    where_ref, order_ref, sequence_ref, q_ref, acc_in, m_in = refs[:6]
+    kv_refs = refs[6 : 6 + n_kv]
+    o_refs = refs[6 + n_kv : 6 + n_kv + n_out]
+    acc_ref, run_ref, kv_ref, slot_ref, list_ref, rank_ref = refs[6 + n_kv + n_out :]
     step = pl.program_id(0)
     first = where_ref[1]
     last = first + where_ref[2]
@@ -125,7 +127,7 @@
                 for j in range(piece_ref.shape[0]):
                     kv_ref[j] = piece_ref[j]
 
-    p = order_ref[where_ref[0] + step]
+    p = order_ref[where_ref[0] + sequence_ref[step]]
     acc_ref[...] = acc_in[0]
     if n_far:
         count = rank_ref[p]
@@ -169,9 +171,13 @@
 
             lax.fori_loop(0, piece_ref.shape[0], careful, 0)
 
-    result = acc_ref[:HD] * (1.0 / acc_ref[HD : HD + 1])
-    for g in range(GROUP):
-        o_ref[:, g * HD : (g + 1) * HD] = result[:, g * SPAN : (g + 1) * SPAN].T.astype(o_ref.dtype)
+    for index, o_ref in enumerate(o_refs):
+
+        @pl.when(jnp.logical_or(n_out == 1, step == index))
+        def _(o_ref=o_ref):
+            result = acc_ref[:HD] * (1.0 / acc_ref[HD : HD + 1])
+            for g in range(GROUP):
+                o_ref[:, g * HD : (g + 1) * HD] = result[:, g * SPAN : (g + 1) * SPAN].T.astype(o_ref.dtype)
 
 
 def attention(q, near, far, near_bases, far_bases, far_first, far_count, first_span, span_order):
@@ -210,25 +216,66 @@
         cost_estimate=cost(0.75),
         name="near",
     )(where, span_order, q, *near)
+
+    def finish(sequence, count, apart):
+        q_block = pl.BlockSpec((SPAN, GROUP * HD), lambda i, w, o, seq: (seq[i], 0))
+        acc_block = pl.BlockSpec((1, HD + EXTRA, ROWS), lambda i, w, o, seq: (seq[i], 0, 0))
+        m_block = pl.BlockSpec((1, 8, ROWS), lambda i, w, o, seq: (seq[i], 0, 0))
+        if apart:
+            out_specs = [pl.BlockSpec((SPAN, GROUP * HD), lambda i, *_: (0, 0))] * count
+            out_shape = [jax.ShapeDtypeStruct((SPAN, GROUP * HD), q.dtype)] * count
+        else:
+            out_specs, out_shape = [q_block], [jax.ShapeDtypeStruct(q.shape, q.dtype)]
+        return pl.pallas_call(
+            functools.partial(far_kernel, len(near) + len(far), len(far), len(out_shape)),
+            grid_spec=pltpu.PrefetchScalarGridSpec(
+                num_scalar_prefetch=3,
+                grid=(count,),
+                in_specs=[q_block, acc_block, m_block] + piece_specs,
+                out_specs=out_specs,
+                scratch_shapes=[
+                    pltpu.VMEM((HD + EXTRA, ROWS), jnp.float32),
+                    pltpu.VMEM((8, ROWS), jnp.float32),
+                    pltpu.VMEM((near[0].shape[0], SPAN + HD, SPAN), jnp.bfloat16),
+                    *lists,
+                ],
+            ),
+            out_shape=out_shape,
+            compiler_params=limit,
+            cost_estimate=cost(0.25 * count / q_spans),
+            name="far",
+        )(where, span_order, sequence, q, acc, m, *near, *far)
+
+    return finish
+
+
+def unpack_kernel(me_ref, *refs):
+    o_ref = refs[-1]
+    for index, part_ref in enumerate(refs[:-1]):
+        column = pl.multiple_of((me_ref[0] ^ index) * GROUP * HD, GROUP * HD)
+        o_ref[:, pl.ds(column, GROUP * HD)] = part_ref[...]
+
+
+def to_token_owners(finish, q_spans):
+    me = lax.axis_index(GROUP_AXES)
+    parts = [None] * KVH
+    for steps in PARTS:
+        sequence = jnp.stack([me ^ step for step in steps]).astype(jnp.int32)
+        for step, done in zip(steps, finish(sequence, len(steps), True)):
+            if step:
+                done = lax.ppermute(done, GROUP_AXES, [(i, i ^ step) for i in range(KVH)])
+            parts[step] = done
     return pl.pallas_call(
-        functools.partial(far_kernel, len(near) + len(far), len(far)),
+        unpack_kernel,
         grid_spec=pltpu.PrefetchScalarGridSpec(
-            num_scalar_prefetch=2,
-            grid=(q_spans,),
-            in_specs=[q_spec, acc_spec, m_spec] + piece_specs,
-            out_specs=q_spec,
-            scratch_shapes=[
-                pltpu.VMEM((HD + EXTRA, ROWS), jnp.float32),
-                pltpu.VMEM((8, ROWS), jnp.float32),
-                pltpu.VMEM((near[0].shape[0], SPAN + HD, SPAN), jnp.bfloat16),
-                *lists,
-            ],
+            num_scalar_prefetch=1,
+            grid=(1,),
+            in_specs=[pl.BlockSpec((SPAN, GROUP * HD), lambda i, *_: (0, 0))] * KVH,
+            out_specs=pl.BlockSpec((SPAN, HQ * HD), lambda i, *_: (0, 0)),
         ),
-        out_shape=jax.ShapeDtypeStruct(q.shape, q.dtype),
-        compiler_params=limit,
-        cost_estimate=cost(0.25),
-        name="far",
-    )(where, span_order, q, acc, m, *near, *far)
+        out_shape=jax.ShapeDtypeStruct((SPAN, HQ * HD), parts[0].dtype),
+        name="unpack",
+    )(me.reshape(1).astype(jnp.int32), *parts)
 
 
 def pack_kernel(k_ref, v_ref, o_ref):
@@ -275,7 +322,10 @@
         near = [lax.all_gather(own, "outer", axis=0, tiled=True)]
         near_bases = [jnp.int32(0)]
         far, far_bases, far_first, far_count = [], [], jnp.int32(0), jnp.int32(0)
-    out = attention(q, near, far, near_bases, far_bases, far_first, far_count, place * group_spans, span_order)
+    finish = attention(q, near, far, near_bases, far_bases, far_first, far_count, place * group_spans, span_order)
+    if rows == SPAN:
+        return to_token_owners(finish, group_spans)
+    out = finish(jnp.arange(group_spans, dtype=jnp.int32), group_spans, False)[0]
     out = lax.all_to_all(out.reshape(KVH, rows, GROUP * HD), GROUP_AXES, split_axis=0, concat_axis=0, tiled=False)
     return out.transpose(1, 0, 2).reshape(rows, HQ * HD)
 

time: 117 us -> 110 us (0.940)
  the two profiles are of different devices: /device:TPU:25 before, /device:TPU:11 now
where the time goes in v1:
time: 110 us; the launch traced here: 112 us
  Pallas kernels  43.6 us (40%)
  waiting for transfers between devices  38.2 us (35%)
  starting transfers between devices  26.8 us (24%)
  local copies, waits for them, and re-layouts  3.01 us (3%)
    pallas_call x1, Pallas kernels, attention(): pl.pallas_call(functools.partial(near_kernel, len(near)), grid_spec=pltpu...  24.2 us
    pallas_call x2, Pallas kernels, finish(): pl.pallas_call(functools.partial(far_kernel, len(near) + len(far), len(fa...  14.3 us
    ppermute x7, waiting for transfers between devices, to_token_owners(): done = lax.ppermute(done, GROUP_AXES, [(i, i ^ step) for i in range(KVH)])  11.6 us
    ppermute x1, waiting for transfers between devices, shards(): lax.ppermute(own, 'outer', [(i, (i + 1) % outer) for i in range(outer)])  11.5 us
    ppermute x7, starting transfers between devices, to_token_owners(): done = lax.ppermute(done, GROUP_AXES, [(i, i ^ step) for i in range(KVH)])  9.55 us
    ppermute x1, waiting for transfers between devices, shards(): lax.ppermute(own, 'outer', [(i, (i - 1) % outer) for i in range(outer)])  8.77 us
    all_to_all x1, waiting for transfers between devices, to_head_owners(): return exchange(packed)  6.25 us
    all_to_all x1, starting transfers between devices, shards(): lax.all_to_all(q, GROUP_AXES, split_axis=0, concat_axis=0, tiled=False)  5.13 us
  transfers between devices with their start and end apart: 13, of which 8 were waited for; matrix products, arithmetic and copies ran while one was open for 2% of the time, Pallas kernels for 28%

profile of v1, /device:TPU:11, one launch (start us, length us, event | category | flops | bytes accessed | tf_op | source)
XLA Modules:
  0.0 111.8 jit_solution(194246572860773833)
XLA Ops:
  0.0 0.0 copy-start.2
  0.0 2.1 %pack.1 = bf16[8,256,128]{2,1,0:T(8,128)(2,1)} custom-call(bf16[128,1024]{1,0:T(8,128)(2,1)} %k_ref.1, bf16[128,1024]{1,0:T(8,128)(2,1)} %v_ref.1), custom_call_target="tpu_custom_call" | custom-call | tf_op jit(solution)/shard_map/pack/pallas_call | solution.py:293
  2.1 4.6 %all-to-all-start.1 = ((bf16[8,256,128]{2,1,0:T(8,128)(2,1)}), bf16[8,256,128]{2,1,0:T(8,128)(2,1)S(1)}, u32[]{:S(2)}, u32[]{:S(2)}) async-start(bf16[8,256,128]{2,1,0:T(8,128)(2,1)} %pack.1), calls=%async_computation.1 | async-start | bytes 1048576 | tf_op jit(solution)/shard_map/all_to_all | solution.py:296
  6.7 0.0 copy-done.2
  6.7 1.5 %copy.8 = bf16[16,8,8,1024]{3,2,0,1:T(8,128)(2,1)} copy(bf16[16,8,8,1024]{3,2,1,0:T(8,128)(2,1)S(1)} %bitcast.27) | data formatting | bytes 4194304 | tf_op jit(solution)/shard_map/reshape | solution.py:308
  8.2 6.2 %all-to-all-done.1.refs_3_.refs_6_ = bf16[8,256,128]{2,1,0:T(8,128)(2,1)S(1)} async-done(((bf16[8,256,128]{2,1,0:T(8,128)(2,1)}), bf16[8,256,128]{2,1,0:T(8,128)(2,1)S(1)}, u32[]{:S(2)}, u32[]{:S(2)}) %all-to-all-start.1) | async-done | bytes 524320 | tf_op jit(solution)/shard_map/all_to_all | solution.py:296
  14.5 0.0 copy-start.1
  14.5 5.1 %all-to-all-start = ((bf16[8,128,1024]{2,1,0:T(8,128)(2,1)}), bf16[8,128,1024]{2,1,0:T(8,128)(2,1)S(1)}, u32[]{:S(2)}, u32[]{:S(2)}) async-start(bf16[8,128,1024]{2,1,0:T(8,128)(2,1)} %bitcast.26), calls=%async_computation | async-start | bytes 4194304 | tf_op jit(solution)/shard_map/all_to_all | solution.py:309
  19.6 1.3 %collective-permute-start = (bf16[8,256,128]{2,1,0:T(8,128)(2,1)S(1)}, bf16[8,256,128]{2,1,0:T(8,128)(2,1)S(1)}, u32[]{:S(2)}, u32[]{:S(2)}) collective-permute-start(bf16[8,256,128]{2,1,0:T(8,128)(2,1)S(1)} %all-to-all-done.1.refs_3_.refs_6_), channel_id=1, source_target_pairs={{0,8},{8,16},{16,24},{24,0},{1,9},{9,17},{17,25},{25,1},{2,10},{10... | collective-permute-start | bytes 1572872 | tf_op jit(solution)/shard_map/ppermute | solution.py:311
  20.9 0.2 collective-permute-start.1
  21.1 0.1 stack.59.refs_0_
  21.1 0.1 pad_add_fusion.1.refs_2_
  21.2 11.5 %collective-permute-done.refs_4_.refs_7_ = bf16[8,256,128]{2,1,0:T(8,128)(2,1)S(1)} collective-permute-done((bf16[8,256,128]{2,1,0:T(8,128)(2,1)S(1)}, bf16[8,256,128]{2,1,0:T(8,128)(2,1)S(1)}, u32[]{:S(2)}, u32[]{:S(2)}) %collective-permute-start) | collective-permute-done | bytes 524320 | tf_op jit(solution)/shard_map/ppermute | solution.py:311
  32.7 4.1 %collective-permute-start.2 = (bf16[8,256,128]{2,1,0:T(8,128)(2,1)S(1)}, bf16[8,256,128]{2,1,0:T(8,128)(2,1)}, u32[]{:S(2)}, u32[]{:S(2)}) collective-permute-start(bf16[8,256,128]{2,1,0:T(8,128)(2,1)S(1)} %collective-permute-done.refs_4_.refs_7_), channel_id=1, source_target_pairs={{8,16},{16,24},{9,17},{17,25},{10,18},{18,26},{11,19},{19,27},{12,... | collective-permute-start | bytes 1572872 | tf_op jit(solution)/shard_map/ppermute | solution.py:313
  36.9 8.8 %collective-permute-done.1.refs_5_.refs_8_ = bf16[8,256,128]{2,1,0:T(8,128)(2,1)} collective-permute-done((bf16[8,256,128]{2,1,0:T(8,128)(2,1)S(1)}, bf16[8,256,128]{2,1,0:T(8,128)(2,1)}, u32[]{:S(2)}, u32[]{:S(2)}) %collective-permute-start.1) | collective-permute-done | bytes 524320 | tf_op jit(solution)/shard_map/ppermute | solution.py:312
  45.6 1.9 %collective-permute-start.3 = (bf16[8,256,128]{2,1,0:T(8,128)(2,1)}, bf16[8,256,128]{2,1,0:T(8,128)(2,1)}, u32[]{:S(2)}, u32[]{:S(2)}) collective-permute-start(bf16[8,256,128]{2,1,0:T(8,128)(2,1)} %collective-permute-done.1.refs_5_.refs_8_), channel_id=1, source_target_pairs={{8,0},{16,8},{9,1},{17,9},{10,2},{18,10},{11,3},{19,11},{12,4},{20... | collective-permute-start | bytes 1572872 | tf_op jit(solution)/shard_map/ppermute | solution.py:314
  47.6 0.0 all-to-all-done
  47.6 0.0 copy-done.1
  47.6 24.2 %near.1 = (f32[8,144,1024]{2,1,0:T(8,128)S(1)}, f32[8,8,1024]{2,1,0:T(8,128)S(1)}) custom-call(s32[8]{0:T(128)S(1)} %stack.59.refs_0_, s32[32]{0:T(128)S(1)} %copy-done.1, bf16[1024,1024]{1,0:T(8,128)(2,1)S(1)} %bitcast.23, bf16[8,256,128]{2,1,0:T(8,128)(2,1)S(1)} %all-to-all-done.1.refs_3_.refs_6_, ...), custom_call_target="tpu_custom_call" | custom-call | flops 12884901888 | bytes 6291456 | tf_op jit(solution)/shard_map/near/pallas_call | solution.py:202
  71.8 0.0 collective-permute-done.2.refs_9_
  71.8 0.0 collective-permute-done.3.refs_10_
  71.8 6.9 %far.3 = (bf16[128,1024]{1,0:T(8,128)(2,1)S(1)}, bf16[128,1024]{1,0:T(8,128)(2,1)S(1)}, bf16[128,1024]{1,0:T(8,128)(2,1)S(1)}, bf16[128,1024]{1,0:T(8,128)(2,1)S(1)}) custom-call(s32[8]{0:T(128)S(1)} %stack.59.refs_0_, s32[32]{0:T(128)S(1)} %copy-done.1, s32[4]{0:T(128)S(1)} %pad_add_fusion.1.refs_2_, bf16[1024,1024]{1,0:T(8,128)(2,1)S(1)} %bitcast.24, ...), custom_call_target="tpu_custom_call" | custom-call | flops 2147483648 | bytes 6291456 | tf_op jit(solution)/shard_map/far/pallas_call | solution.py:229
  78.8 5.4 %collective-permute-start.10 = (bf16[128,1024]{1,0:T(8,128)(2,1)S(1)}, bf16[128,1024]{1,0:T(8,128)(2,1)S(1)}, u32[]{:S(2)}, u32[]{:S(2)}) collective-permute-start(bf16[128,1024]{1,0:T(8,128)(2,1)S(1)} %get-tuple-element.24), channel_id=1, source_target_pairs={{0,7},{1,6},{2,5},{3,4},{4,3},{5,2},{6,1},{7,0},{8,15},{9,14},{10,... | collective-permute-start | bytes 786440 | tf_op jit(solution)/shard_map/ppermute | solution.py:266
  84.2 1.1 %collective-permute-start.4 = (bf16[128,1024]{1,0:T(8,128)(2,1)S(1)}, bf16[128,1024]{1,0:T(8,128)(2,1)S(1)}, u32[]{:S(2)}, u32[]{:S(2)}) collective-permute-start(bf16[128,1024]{1,0:T(8,128)(2,1)S(1)} %get-tuple-element.18), channel_id=1, source_target_pairs={{0,1},{1,0},{2,3},{3,2},{4,5},{5,4},{6,7},{7,6},{8,9},{9,8},{10,11... | collective-permute-start | bytes 786440 | tf_op jit(solution)/shard_map/ppermute | solution.py:266
  85.3 0.1 pad_add_fusion.refs_2_
  85.4 0.5 collective-permute-start.7
  85.9 1.0 collective-permute-start.8
  86.9 7.4 %far.2 = (bf16[128,1024]{1,0:T(8,128)(2,1)S(1)}, bf16[128,1024]{1,0:T(8,128)(2,1)S(1)}, bf16[128,1024]{1,0:T(8,128)(2,1)S(1)}, bf16[128,1024]{1,0:T(8,128)(2,1)S(1)}) custom-call(s32[8]{0:T(128)S(1)} %stack.59.refs_0_, s32[32]{0:T(128)S(1)} %copy-done.1, s32[4]{0:T(128)S(1)} %pad_add_fusion.refs_2_, bf16[1024,1024]{1,0:T(8,128)(2,1)S(1)} %bitcast.25, ...), custom_call_target="tpu_custom_call" | custom-call | flops 2147483648 | bytes 6291456 | tf_op jit(solution)/shard_map/far/pallas_call | solution.py:229
  94.3 0.0 copy-start
  94.3 0.7 copy-done
  95.0 0.0 collective-permute-start.5
  95.0 0.0 collective-permute-done.10.refs_7_
  95.0 0.0 copy-start.3
  95.0 1.5 %collective-permute-start.6 = (bf16[128,1024]{1,0:T(8,128)(2,1)S(1)}, bf16[128,1024]{1,0:T(8,128)(2,1)S(1)}, u32[]{:S(2)}, u32[]{:S(2)}) collective-permute-start(bf16[128,1024]{1,0:T(8,128)(2,1)S(1)} %get-tuple-element.20), channel_id=1, source_target_pairs={{0,3},{1,2},{2,1},{3,0},{4,7},{5,6},{6,5},{7,4},{8,11},{9,10},{10,... | collective-permute-start | bytes 786440 | tf_op jit(solution)/shard_map/ppermute | solution.py:266
  96.5 1.3 %collective-permute-done.4.refs_1_ = bf16[128,1024]{1,0:T(8,128)(2,1)S(1)} collective-permute-done((bf16[128,1024]{1,0:T(8,128)(2,1)S(1)}, bf16[128,1024]{1,0:T(8,128)(2,1)S(1)}, u32[]{:S(2)}, u32[]{:S(2)}) %collective-permute-start.4) | collective-permute-done | bytes 262176 | tf_op jit(solution)/shard_map/ppermute | solution.py:266
  97.8 0.0 copy-start.4
  97.8 0.0 collective-permute-start.9
  97.9 0.1 collective-permute-done.7.refs_4_
  97.9 0.0 copy-start.5
  97.9 5.5 %collective-permute-done.8.refs_5_ = bf16[128,1024]{1,0:T(8,128)(2,1)S(1)} collective-permute-done((bf16[128,1024]{1,0:T(8,128)(2,1)S(1)}, bf16[128,1024]{1,0:T(8,128)(2,1)S(1)}, u32[]{:S(2)}, u32[]{:S(2)}) %collective-permute-start.8) | collective-permute-done | bytes 262176 | tf_op jit(solution)/shard_map/ppermute | solution.py:266
  103.4 0.0 copy-start.6
  103.4 0.0 collective-permute-done.5.refs_2_
  103.4 0.0 copy-start.7
  103.4 3.1 %collective-permute-done.6.refs_3_ = bf16[128,1024]{1,0:T(8,128)(2,1)S(1)} collective-permute-done((bf16[128,1024]{1,0:T(8,128)(2,1)S(1)}, bf16[128,1024]{1,0:T(8,128)(2,1)S(1)}, u32[]{:S(2)}, u32[]{:S(2)}) %collective-permute-start.6) | collective-permute-done | bytes 262176 | tf_op jit(solution)/shard_map/ppermute | solution.py:266
  106.5 0.0 copy-start.8
  106.5 1.6 %collective-permute-done.9.refs_6_ = bf16[128,1024]{1,0:T(8,128)(2,1)S(1)} collective-permute-done((bf16[128,1024]{1,0:T(8,128)(2,1)S(1)}, bf16[128,1024]{1,0:T(8,128)(2,1)S(1)}, u32[]{:S(2)}, u32[]{:S(2)}) %collective-permute-start.9) | collective-permute-done | bytes 262176 | tf_op jit(solution)/shard_map/ppermute | solution.py:266
  108.1 0.0 copy-done.4
  108.1 0.0 copy-done.5
  108.1 0.0 copy-done.6
  108.1 0.0 copy-start.9
  108.2 0.0 copy-done.3
  108.2 0.0 copy-done.7
  108.2 0.0 copy-done.8
  108.2 0.7 copy-done.9
  108.9 3.0 %unpack.1 = bf16[128,8192]{1,0:T(8,128)(2,1)} custom-call(s32[1]{0:T(128)} %bitcast.me_ref, bf16[128,1024]{1,0:T(8,128)(2,1)} %copy-done, bf16[128,1024]{1,0:T(8,128)(2,1)} %copy-done.4, bf16[128,1024]{1,0:T(8,128)(2,1)} %copy-done.7, bf16[128,1024]{1,0:T(8,128)(2,1)} %copy-done.8, bf16[128,1024]{1,0:T(8,128)(2,1)} %copy-done.5, ...), custom_call_target="tpu_custom_call" | custom-call | tf_op jit(solution)/shard_map/unpack/pallas_call | solution.py:268
Async XLA Ops:
  0.0 6.7 %copy-start.2 = (bf16[128,8192]{1,0:T(8,128)(2,1)S(1)}, bf16[128,8192]{1,0:T(8,128)(2,1)}, u32[]{:S(2)}) copy-start(bf16[128,8192]{1,0:T(8,128)(2,1)} %param.4) | copy-start | bytes 6291460
  2.1 12.3 %all-to-all-start.1 = ((bf16[8,256,128]{2,1,0:T(8,128)(2,1)}), bf16[8,256,128]{2,1,0:T(8,128)(2,1)S(1)}, u32[]{:S(2)}, u32[]{:S(2)}) async-start(bf16[8,256,128]{2,1,0:T(8,128)(2,1)} %pack.1), calls=%async_computation.1 | async-start | bytes 1048576 | tf_op jit(solution)/shard_map/all_to_all | solution.py:296
  14.5 33.1 %copy-start.1 = (s32[32]{0:T(128)S(1)}, s32[32]{0:T(128)}, u32[]{:S(2)}) copy-start(s32[32]{0:T(128)} %refs_1_.5) | copy-start | bytes 388
  14.5 33.1 %all-to-all-start = ((bf16[8,128,1024]{2,1,0:T(8,128)(2,1)}), bf16[8,128,1024]{2,1,0:T(8,128)(2,1)S(1)}, u32[]{:S(2)}, u32[]{:S(2)}) async-start(bf16[8,128,1024]{2,1,0:T(8,128)(2,1)} %bitcast.26), calls=%async_computation | async-start | bytes 4194304 | tf_op jit(solution)/shard_map/all_to_all | solution.py:309
  19.6 13.1 %collective-permute-start = (bf16[8,256,128]{2,1,0:T(8,128)(2,1)S(1)}, bf16[8,256,128]{2,1,0:T(8,128)(2,1)S(1)}, u32[]{:S(2)}, u32[]{:S(2)}) collective-permute-start(bf16[8,256,128]{2,1,0:T(8,128)(2,1)S(1)} %all-to-all-done.1.refs_3_.refs_6_), channel_id=1, source_target_pairs={{0,8},{8,16},{16,24},{24,0},{1,9},{9,17},{17,25},{25,1},{2,10},{10... | collective-permute-start | bytes 1572872 | tf_op jit(solution)/shard_map/ppermute | solution.py:311
  20.9 24.7 %collective-permute-start.1 = (bf16[8,256,128]{2,1,0:T(8,128)(2,1)S(1)}, bf16[8,256,128]{2,1,0:T(8,128)(2,1)}, u32[]{:S(2)}, u32[]{:S(2)}) collective-permute-start(bf16[8,256,128]{2,1,0:T(8,128)(2,1)S(1)} %all-to-all-done.1.refs_3_.refs_6_), channel_id=1, source_target_pairs={{0,24},{8,0},{16,8},{24,16},{1,25},{9,1},{17,9},{25,17},{2,26},{10... | collective-permute-start | bytes 1572872 | tf_op jit(solution)/shard_map/ppermute | solution.py:312
  32.7 39.0 %collective-permute-start.2 = (bf16[8,256,128]{2,1,0:T(8,128)(2,1)S(1)}, bf16[8,256,128]{2,1,0:T(8,128)(2,1)}, u32[]{:S(2)}, u32[]{:S(2)}) collective-permute-start(bf16[8,256,128]{2,1,0:T(8,128)(2,1)S(1)} %collective-permute-done.refs_4_.refs_7_), channel_id=1, source_target_pairs={{8,16},{16,24},{9,17},{17,25},{10,18},{18,26},{11,19},{19,27},{12,... | collective-permute-start | bytes 1572872 | tf_op jit(solution)/shard_map/ppermute | solution.py:313
  45.6 26.2 %collective-permute-start.3 = (bf16[8,256,128]{2,1,0:T(8,128)(2,1)}, bf16[8,256,128]{2,1,0:T(8,128)(2,1)}, u32[]{:S(2)}, u32[]{:S(2)}) collective-permute-start(bf16[8,256,128]{2,1,0:T(8,128)(2,1)} %collective-permute-done.1.refs_5_.refs_8_), channel_id=1, source_target_pairs={{8,0},{16,8},{9,1},{17,9},{10,2},{18,10},{11,3},{19,11},{12,4},{20... | collective-permute-start | bytes 1572872 | tf_op jit(solution)/shard_map/ppermute | solution.py:314
  78.8 16.3 %collective-permute-start.10 = (bf16[128,1024]{1,0:T(8,128)(2,1)S(1)}, bf16[128,1024]{1,0:T(8,128)(2,1)S(1)}, u32[]{:S(2)}, u32[]{:S(2)}) collective-permute-start(bf16[128,1024]{1,0:T(8,128)(2,1)S(1)} %get-tuple-element.24), channel_id=1, source_target_pairs={{0,7},{1,6},{2,5},{3,4},{4,3},{5,2},{6,1},{7,0},{8,15},{9,14},{10,... | collective-permute-start | bytes 786440 | tf_op jit(solution)/shard_map/ppermute | solution.py:266
  84.2 13.7 %collective-permute-start.4 = (bf16[128,1024]{1,0:T(8,128)(2,1)S(1)}, bf16[128,1024]{1,0:T(8,128)(2,1)S(1)}, u32[]{:S(2)}, u32[]{:S(2)}) collective-permute-start(bf16[128,1024]{1,0:T(8,128)(2,1)S(1)} %get-tuple-element.18), channel_id=1, source_target_pairs={{0,1},{1,0},{2,3},{3,2},{4,5},{5,4},{6,7},{7,6},{8,9},{9,8},{10,11... | collective-permute-start | bytes 786440 | tf_op jit(solution)/shard_map/ppermute | solution.py:266
  85.4 12.5 %collective-permute-start.7 = (bf16[128,1024]{1,0:T(8,128)(2,1)S(1)}, bf16[128,1024]{1,0:T(8,128)(2,1)S(1)}, u32[]{:S(2)}, u32[]{:S(2)}) collective-permute-start(bf16[128,1024]{1,0:T(8,128)(2,1)S(1)} %get-tuple-element.21), channel_id=1, source_target_pairs={{0,4},{1,5},{2,6},{3,7},{4,0},{5,1},{6,2},{7,3},{8,12},{9,13},{10,... | collective-permute-start | bytes 786440 | tf_op jit(solution)/shard_map/ppermute | solution.py:266
  85.9 17.5 %collective-permute-start.8 = (bf16[128,1024]{1,0:T(8,128)(2,1)S(1)}, bf16[128,1024]{1,0:T(8,128)(2,1)S(1)}, u32[]{:S(2)}, u32[]{:S(2)}) collective-permute-start(bf16[128,1024]{1,0:T(8,128)(2,1)S(1)} %get-tuple-element.22), channel_id=1, source_target_pairs={{0,5},{1,4},{2,7},{3,6},{4,1},{5,0},{6,3},{7,2},{8,13},{9,12},{10,... | collective-permute-start | bytes 786440 | tf_op jit(solution)/shard_map/ppermute | solution.py:266
  94.3 0.7 copy-start
  95.0 8.4 %collective-permute-start.5 = (bf16[128,1024]{1,0:T(8,128)(2,1)S(1)}, bf16[128,1024]{1,0:T(8,128)(2,1)S(1)}, u32[]{:S(2)}, u32[]{:S(2)}) collective-permute-start(bf16[128,1024]{1,0:T(8,128)(2,1)S(1)} %get-tuple-element.19), channel_id=1, source_target_pairs={{0,2},{1,3},{2,0},{3,1},{4,6},{5,7},{6,4},{7,5},{8,10},{9,11},{10,... | collective-permute-start | bytes 786440 | tf_op jit(solution)/shard_map/ppermute | solution.py:266
  95.0 13.1 %copy-start.3 = (bf16[128,1024]{1,0:T(8,128)(2,1)}, bf16[128,1024]{1,0:T(8,128)(2,1)S(1)}, u32[]{:S(2)}) copy-start(bf16[128,1024]{1,0:T(8,128)(2,1)S(1)} %collective-permute-done.10.refs_7_) | copy-start | bytes 786436
  95.0 11.5 %collective-permute-start.6 = (bf16[128,1024]{1,0:T(8,128)(2,1)S(1)}, bf16[128,1024]{1,0:T(8,128)(2,1)S(1)}, u32[]{:S(2)}, u32[]{:S(2)}) collective-permute-start(bf16[128,1024]{1,0:T(8,128)(2,1)S(1)} %get-tuple-element.20), channel_id=1, source_target_pairs={{0,3},{1,2},{2,1},{3,0},{4,7},{5,6},{6,5},{7,4},{8,11},{9,10},{10,... | collective-permute-start | bytes 786440 | tf_op jit(solution)/shard_map/ppermute | solution.py:266
  97.8 10.3 %copy-start.4 = (bf16[128,1024]{1,0:T(8,128)(2,1)}, bf16[128,1024]{1,0:T(8,128)(2,1)S(1)}, u32[]{:S(2)}) copy-start(bf16[128,1024]{1,0:T(8,128)(2,1)S(1)} %collective-permute-done.4.refs_1_) | copy-start | bytes 786436
  97.8 10.3 %collective-permute-start.9 = (bf16[128,1024]{1,0:T(8,128)(2,1)S(1)}, bf16[128,1024]{1,0:T(8,128)(2,1)S(1)}, u32[]{:S(2)}, u32[]{:S(2)}) collective-permute-start(bf16[128,1024]{1,0:T(8,128)(2,1)S(1)} %get-tuple-element.23), channel_id=1, source_target_pairs={{0,6},{1,7},{2,4},{3,5},{4,2},{5,3},{6,0},{7,1},{8,14},{9,15},{10,... | collective-permute-start | bytes 786440 | tf_op jit(solution)/shard_map/ppermute | solution.py:266
  97.9 10.2 %copy-start.5 = (bf16[128,1024]{1,0:T(8,128)(2,1)}, bf16[128,1024]{1,0:T(8,128)(2,1)S(1)}, u32[]{:S(2)}) copy-start(bf16[128,1024]{1,0:T(8,128)(2,1)S(1)} %collective-permute-done.7.refs_4_) | copy-start | bytes 786436
  103.4 4.8 %copy-start.6 = (bf16[128,1024]{1,0:T(8,128)(2,1)}, bf16[128,1024]{1,0:T(8,128)(2,1)S(1)}, u32[]{:S(2)}) copy-start(bf16[128,1024]{1,0:T(8,128)(2,1)S(1)} %collective-permute-done.8.refs_5_) | copy-start | bytes 786436
  103.4 4.8 %copy-start.7 = (bf16[128,1024]{1,0:T(8,128)(2,1)}, bf16[128,1024]{1,0:T(8,128)(2,1)S(1)}, u32[]{:S(2)}) copy-start(bf16[128,1024]{1,0:T(8,128)(2,1)S(1)} %collective-permute-done.5.refs_2_) | copy-start | bytes 786436
  106.5 1.7 %copy-start.8 = (bf16[128,1024]{1,0:T(8,128)(2,1)}, bf16[128,1024]{1,0:T(8,128)(2,1)S(1)}, u32[]{:S(2)}) copy-start(bf16[128,1024]{1,0:T(8,128)(2,1)S(1)} %collective-permute-done.6.refs_3_) | copy-start | bytes 786436
  108.1 0.7 copy-start.9

commit v2 on v1

v2 whole, which is shorter than its diff:
```python
import functools
import math

import jax
import jax.numpy as jnp
from jax import lax
from jax.experimental import pallas as pl
from jax.experimental.pallas import tpu as pltpu
from jax.sharding import Mesh
from jax.sharding import PartitionSpec as P

HQ = 64
KVH = 8
HD = 128
SPAN = 128
GROUP = HQ // KVH
ROWS = GROUP * SPAN
SCALE = HD**-0.5 * math.log2(math.e)
EXTRA = 16
BLOCK = 8
VMEM = 24 * 2**20
NT = (((1,), (1,)), ((), ()))
GROUP_AXES = ("inner", "head")
PARTS = ((5, 7), (1, 4, 3), (6, 2, 0))


def queries_of(q_ref):
    return jnp.concatenate([q_ref[:, g * HD : (g + 1) * HD] for g in range(GROUP)], 0)


def scores(keys, q_ref):
    return lax.dot_general(keys, queries_of(q_ref), NT, preferred_element_type=jnp.float32) * SCALE


def blend(values, weights):
    ones = jnp.ones((EXTRA, values.shape[1]), jnp.bfloat16)
    values = jnp.concatenate([values, ones], 0)
    return jnp.dot(values, weights.astype(jnp.bfloat16), preferred_element_type=jnp.float32)


def causal(s):
    key = lax.broadcasted_iota(jnp.int32, (SPAN, ROWS), 0)
    row = lax.broadcasted_iota(jnp.int32, (SPAN, ROWS), 1) % SPAN
    return jnp.where(key <= row, s, -1e30)


def gather(kv_ref, slots):
    return (
        jnp.concatenate([kv_ref[s, :SPAN] for s in slots], 0),
        jnp.concatenate([kv_ref[s, SPAN:] for s in slots], 1),
    )


def listing(order, wanted):
    n = order.shape[0]
    numbers = jnp.arange(n, dtype=jnp.int32)
    before = jnp.logical_and(order[None, :] < order[:, None], wanted[None, :])
    rank = jnp.sum(before.astype(jnp.int32), axis=1)
    mine = jnp.logical_and(rank[None, :] == numbers[:, None], wanted[None, :])
    return rank, jnp.sum(jnp.where(mine, numbers[None, :], 0), axis=1)


class Table:
    def __init__(self, spans):
        self.first, self.far_first, self.bases = 0, 1, 2
        self.order = 16
        self.near_rank, self.near_list, self.far_rank, self.far_list = (16 + spans * (1 + t) for t in range(4))
        self.sequence = 16 + spans * 5


def near_kernel(at, n_kv, *refs):
    t_ref, q_ref = refs[:2]
    pieces = refs[2 : 2 + n_kv]
    acc_ref, m_ref, kv_ref, sems = refs[2 + n_kv :]
    step = pl.program_id(0)

    @pl.when(step == 0)
    def _():
        copies = [
            pltpu.make_async_copy(
                piece, kv_ref.at[pl.ds(t_ref[at.bases + index], piece.shape[0])], sems.at[index]
            )
            for index, piece in enumerate(pieces)
        ]
        for copy in copies:
            copy.start()
        for copy in copies:
            copy.wait()

    rank = t_ref[at.near_rank + t_ref[at.first] + step]

    def first_block(count):
        start = at.near_list + rank + 1 - count
        keys, values = gather(kv_ref, [t_ref[start + t] for t in range(count)])
        s = scores(keys, q_ref)
        own = causal(s[(count - 1) * SPAN :])
        s = jnp.concatenate([s[: (count - 1) * SPAN], own], 0) if count > 1 else own
        m = jnp.max(s, axis=0, keepdims=True)
        m_ref[0] = jnp.broadcast_to(m, m_ref.shape[1:])
        acc_ref[0] = blend(values, jnp.exp2(s - m))

    for count in range(1, BLOCK + 1):

        @pl.when(rank % BLOCK == count - 1)
        def _(count=count):
            first_block(count)

    def block(b, carry):
        keys, values = gather(kv_ref, [t_ref[at.near_list + b * BLOCK + t] for t in range(BLOCK)])
        acc_ref[0] += blend(values, jnp.exp2(scores(keys, q_ref) - m_ref[0, :1]))
        return carry

    lax.fori_loop(0, rank // BLOCK, block, 0)


def far_kernel(at, offset, n_kv, n_far, n_out, *refs):
    t_ref, q_ref, acc_in, m_in = refs[:4]
    pieces = refs[4 : 4 + n_kv]
    o_refs = refs[4 + n_kv : 4 + n_kv + n_out]
    acc_ref, run_ref, kv_ref, span_ref, sem = refs[4 + n_kv + n_out :]
    step = pl.program_id(0)
    stored = t_ref[at.first] + t_ref[at.sequence + offset + step]
    p = t_ref[at.order + stored]

    @pl.when(step == 0)
    def _():
        for index in range(n_kv - n_far, n_kv):

            @pl.when(t_ref[at.bases + index] >= 0)
            def _(piece=pieces[index]):
                copy = pltpu.make_async_copy(piece, kv_ref, sem)
                copy.start()
                copy.wait()

    count = t_ref[at.far_rank + stored] if n_far else 0

    @pl.when(count == 0)
    def _():
        acc_ref[...] = acc_in[0]

    for size in range(1, 1 + (kv_ref.shape[0] if n_far else 0)):

        @pl.when(count == size)
        def _(size=size):
            slots = [t_ref[at.far_list + t] - t_ref[at.far_first] for t in range(size)]
            keys, values = gather(kv_ref, slots)
            acc_ref[...] = acc_in[0] + blend(values, jnp.exp2(scores(keys, q_ref) - m_in[0, :1]))

    @pl.when(jnp.logical_not(jnp.max(acc_ref[HD : HD + 8]) < 1e30))
    def _():
        run_ref[...] = jnp.full_like(run_ref, -1e30)
        acc_ref[...] = jnp.zeros_like(acc_ref)
        for index, piece in enumerate(pieces):
            base = t_ref[at.bases + index]

            def careful(j, carry, piece=piece, base=base):
                other = t_ref[at.order + jnp.maximum(base, 0) + j]

                @pl.when(jnp.logical_and(base >= 0, other <= p))
                def _():
                    copy = pltpu.make_async_copy(piece.at[j], span_ref, sem)
                    copy.start()
                    copy.wait()
                    s = scores(span_ref[:SPAN], q_ref)
                    s = jnp.where(other < p, s, causal(s))
                    old = run_ref[...]
                    new = jnp.maximum(old, jnp.max(s, axis=0, keepdims=True))
                    run_ref[...] = new
                    fresh = blend(span_ref[SPAN:], jnp.exp2(s - new[:1]))
                    acc_ref[...] = acc_ref[...] * jnp.exp2(old - new)[:1] + fresh

                return carry

            lax.fori_loop(0, piece.shape[0], careful, 0)

    for index, o_ref in enumerate(o_refs):

        @pl.when(jnp.logical_or(n_out == 1, step == index))
        def _(o_ref=o_ref):
            result = acc_ref[:HD] * (1.0 / acc_ref[HD : HD + 1])
            for g in range(GROUP):
                o_ref[:, g * HD : (g + 1) * HD] = result[:, g * SPAN : (g + 1) * SPAN].T.astype(o_ref.dtype)


def attention(q, near, far, near_bases, far_bases, far_first, first_span, span_order, sequence):
    q_spans = q.shape[0] // SPAN
    spans = span_order.shape[0]
    at = Table(spans)
    numbers = jnp.arange(spans, dtype=jnp.int32)
    if far:
        is_far = jnp.logical_and(numbers >= far_first, numbers < far_first + far[0].shape[0])
    else:
        is_far = numbers < 0
    head = jnp.stack([first_span, far_first, *near_bases, *far_bases]).astype(jnp.int32)
    head = jnp.pad(head, (0, at.order - head.shape[0]))
    near_lists = listing(span_order, jnp.logical_not(is_far))
    table = jnp.concatenate([head, span_order, *near_lists, *listing(span_order, is_far), sequence])
    elements = q.shape[0] * GROUP * spans * SPAN // 2
    limit = pltpu.CompilerParams(vmem_limit_bytes=VMEM)
    anywhere = pl.BlockSpec(memory_space=pl.ANY)

    def cost(part):
        return pl.CostEstimate(
            flops=int(8 * HD * elements * part),
            bytes_accessed=4 * q.size + 4 * spans * SPAN * HD,
            transcendentals=int(elements * part),
        )

    acc, m = pl.pallas_call(
        functools.partial(near_kernel, at, len(near)),
        grid_spec=pltpu.PrefetchScalarGridSpec(
            num_scalar_prefetch=1,
            grid=(q_spans,),
            in_specs=[pl.BlockSpec((SPAN, GROUP * HD), lambda i, t: (i, 0))] + [anywhere] * len(near),
            out_specs=[
                pl.BlockSpec((1, HD + EXTRA, ROWS), lambda i, t: (i, 0, 0)),
                pl.BlockSpec((1, 8, ROWS), lambda i, t: (i, 0, 0)),
            ],
            scratch_shapes=[
                pltpu.VMEM((spans, SPAN + HD, SPAN), jnp.bfloat16),
                pltpu.SemaphoreType.DMA((len(near),)),
            ],
        ),
        out_shape=[
            jax.ShapeDtypeStruct((q_spans, HD + EXTRA, ROWS), jnp.float32),
            jax.ShapeDtypeStruct((q_spans, 8, ROWS), jnp.float32),
        ],
        compiler_params=limit,
        cost_estimate=cost(0.75),
        name="near",
    )(table, q, *near)

    def finish(offset, count, apart):
        def nth(i, t):
            return t[at.sequence + offset + i]

        q_block = pl.BlockSpec((SPAN, GROUP * HD), lambda i, t: (nth(i, t), 0))
        acc_block = pl.BlockSpec((1, HD + EXTRA, ROWS), lambda i, t: (nth(i, t), 0, 0))
        m_block = pl.BlockSpec((1, 8, ROWS), lambda i, t: (nth(i, t), 0, 0))
        if apart:
            out_specs = [pl.BlockSpec((SPAN, GROUP * HD), lambda i, t: (0, 0))] * count
            out_shape = [jax.ShapeDtypeStruct((SPAN, GROUP * HD), q.dtype)] * count
        else:
            out_specs, out_shape = [q_block], [jax.ShapeDtypeStruct(q.shape, q.dtype)]
        n_kv = len(near) + len(far)
        return pl.pallas_call(
            functools.partial(far_kernel, at, offset, n_kv, len(far), len(out_shape)),
            grid_spec=pltpu.PrefetchScalarGridSpec(
                num_scalar_prefetch=1,
                grid=(count,),
                in_specs=[q_block, acc_block, m_block] + [anywhere] * n_kv,
                out_specs=out_specs,
                scratch_shapes=[
                    pltpu.VMEM((HD + EXTRA, ROWS), jnp.float32),
                    pltpu.VMEM((8, ROWS), jnp.float32),
                    pltpu.VMEM((near[0].shape[0], SPAN + HD, SPAN), jnp.bfloat16),
                    pltpu.VMEM((SPAN + HD, SPAN), jnp.bfloat16),
                    pltpu.SemaphoreType.DMA,
                ],
            ),
            out_shape=out_shape,
            compiler_params=limit,
            cost_estimate=cost(0.25 * count / q_spans),
            name="far",
        )(table, q, acc, m, *near, *far)

    return finish


def unpack_kernel(me_ref, *refs):
    o_ref = refs[-1]
    for index, part_ref in enumerate(refs[:-1]):
        column = pl.multiple_of((me_ref[0] ^ index) * GROUP * HD, GROUP * HD)
        o_ref[:, pl.ds(column, GROUP * HD)] = part_ref[...]


def to_token_owners(finish, me):
    parts = [None] * KVH
    offset = 0
    for steps in PARTS:
        for step, done in zip(steps, finish(offset, len(steps), True)):
            if step:
                done = lax.ppermute(done, GROUP_AXES, [(i, i ^ step) for i in range(KVH)])
            parts[step] = done
        offset += len(steps)
    return pl.pallas_call(
        unpack_kernel,
        grid_spec=pltpu.PrefetchScalarGridSpec(
            num_scalar_prefetch=1,
            grid=(1,),
            in_specs=[pl.BlockSpec((SPAN, GROUP * HD), lambda i, *_: (0, 0))] * KVH,
            out_specs=pl.BlockSpec((SPAN, HQ * HD), lambda i, *_: (0, 0)),
        ),
        out_shape=jax.ShapeDtypeStruct((SPAN, HQ * HD), parts[0].dtype),
        compiler_params=pltpu.CompilerParams(vmem_limit_bytes=VMEM),
        name="unpack",
    )(me.reshape(1), *parts)


def pack_kernel(k_ref, v_ref, o_ref):
    for h in range(KVH):
        o_ref[h, :SPAN] = k_ref[:, h * HD : (h + 1) * HD]
        o_ref[h, SPAN:] = v_ref[:, h * HD : (h + 1) * HD].T


def to_head_owners(key_rows, value_rows):
    rows = key_rows.shape[0]
    exchange = functools.partial(
        lax.all_to_all, axis_name=GROUP_AXES, split_axis=0, concat_axis=0, tiled=False
    )
    if rows == SPAN:
        packed = pl.pallas_call(
            pack_kernel, out_shape=jax.ShapeDtypeStruct((KVH, SPAN + HD, SPAN), key_rows.dtype), name="pack",
            compiler_params=pltpu.CompilerParams(vmem_limit_bytes=VMEM),
        )(key_rows, value_rows)
        return exchange(packed)
    packed = jnp.concatenate([key_rows.reshape(rows, KVH, HD), value_rows.reshape(rows, KVH, HD)], 2)
    own = exchange(packed.transpose(1, 0, 2)).reshape(KVH * rows // SPAN, SPAN, 2 * HD)
    return jnp.concatenate([own[:, :, :HD], own[:, :, HD:].transpose(0, 2, 1)], 1)


def shards(outer, queries, key_rows, value_rows, span_order):
    rows = queries.shape[0]
    place = lax.axis_index("outer")
    group_rows = KVH * rows
    group_spans = group_rows // SPAN
    own = to_head_owners(key_rows, value_rows)
    q = queries.reshape(rows, KVH, GROUP * HD).transpose(1, 0, 2)
    q = lax.all_to_all(q, GROUP_AXES, split_axis=0, concat_axis=0, tiled=False).reshape(group_rows, GROUP * HD)
    if outer == 4:
        up = lax.ppermute(own, "outer", [(i, (i + 1) % outer) for i in range(outer)])
        down = lax.ppermute(own, "outer", [(i, (i - 1) % outer) for i in range(outer)])
        far_up = lax.ppermute(up, "outer", [(1, 2), (2, 3)])
        far_down = lax.ppermute(down, "outer", [(1, 0), (2, 1)])
        near = [own, up, down]
        near_bases = [(place + step) % outer * group_spans for step in (0, outer - 1, 1)]
        far = [far_up, far_down]
        far_first = (place + 2) % outer * group_spans
        far_bases = [jnp.where(place >= 2, far_first, -1), jnp.where(place < 2, far_first, -1)]
    else:
        near = [lax.all_gather(own, "outer", axis=0, tiled=True)]
        near_bases = [jnp.int32(0)]
        far, far_bases, far_first = [], [], jnp.int32(0)
    me = lax.axis_index(GROUP_AXES).astype(jnp.int32)
    if rows == SPAN:
        sequence = jnp.stack([me ^ step for steps in PARTS for step in steps])
    else:
        sequence = jnp.arange(group_spans, dtype=jnp.int32)
    finish = attention(q, near, far, near_bases, far_bases, far_first, place * group_spans, span_order, sequence)
    if rows == SPAN:
        return to_token_owners(finish, me)
    out = finish(0, group_spans, False)[0]
    out = lax.all_to_all(out.reshape(KVH, rows, GROUP * HD), GROUP_AXES, split_axis=0, concat_axis=0, tiled=False)
    return out.transpose(1, 0, 2).reshape(rows, HQ * HD)


def solution(mesh):
    ctx, head = mesh.devices.shape
    inner = KVH // head
    split = Mesh(mesh.devices.reshape(ctx // inner, inner, head), ("outer", "inner", "head"))
    spec = P(("outer", "inner", "head"), None)
    return jax.shard_map(
        functools.partial(shards, ctx // inner),
        mesh=split,
        in_specs=(spec, spec, spec, P()),
        out_specs=spec,
        check_vma=False,
    )
```

time: 110 us -> 104 us (0.945)
  the two profiles are of different devices: /device:TPU:11 before, /device:TPU:17 now
where the time goes in v2:
time: 104 us; the launch traced here: 103 us
  Pallas kernels  35.1 us (34%)
  waiting for transfers between devices  35.1 us (34%)
  starting transfers between devices  29 us (28%)
  local copies, waits for them, and re-layouts  3.65 us (4%)
    pallas_call x1, Pallas kernels, attention(): pl.pallas_call(functools.partial(near_kernel, at, len(near)), grid_spec=p...  19.2 us
    pallas_call x3, Pallas kernels, finish(): pl.pallas_call(functools.partial(far_kernel, at, offset, n_kv, len(far),...  13.5 us
    ppermute x1, waiting for transfers between devices, shards(): lax.ppermute(own, 'outer', [(i, (i + 1) % outer) for i in range(outer)])  11.5 us
    ppermute x7, starting transfers between devices, to_token_owners(): done = lax.ppermute(done, GROUP_AXES, [(i, i ^ step) for i in range(KVH)])  11.1 us
    ppermute x7, waiting for transfers between devices, to_token_owners(): done = lax.ppermute(done, GROUP_AXES, [(i, i ^ step) for i in range(KVH)])  8.83 us
    ppermute x1, waiting for transfers between devices, shards(): lax.ppermute(own, 'outer', [(i, (i - 1) % outer) for i in range(outer)])  7.87 us
    all_to_all x1, waiting for transfers between devices, to_head_owners(): return exchange(packed)  6.89 us
    all_to_all x1, starting transfers between devices, shards(): lax.all_to_all(q, GROUP_AXES, split_axis=0, concat_axis=0, tiled=False)  4.46 us
  transfers between devices with their start and end apart: 13, of which 6 were waited for; matrix products, arithmetic and copies ran while one was open for 2% of the time, Pallas kernels for 28%

profile of v2, /device:TPU:17, one launch (start us, length us, event | category | flops | bytes accessed | tf_op | source)
XLA Modules:
  0.0 103.3 jit_solution(16888040371152144722)
XLA Ops:
  0.0 0.0 copy-start
  0.0 0.9 copy-done
  1.0 0.0 copy-start.1
  1.0 0.9 copy-done.1
  1.9 0.0 copy-start.2
  1.9 0.9 pack.1
  2.8 4.4 %all-to-all-start.1 = ((bf16[8,256,128]{2,1,0:T(8,128)(2,1)}), bf16[8,256,128]{2,1,0:T(8,128)(2,1)S(1)}, u32[]{:S(2)}, u32[]{:S(2)}) async-start(bf16[8,256,128]{2,1,0:T(8,128)(2,1)} %pack.1), calls=%async_computation.1 | async-start | bytes 1048576 | tf_op jit(solution)/shard_map/all_to_all | solution.py:316
  7.2 0.0 copy-done.2
  7.2 1.6 %copy.9 = bf16[16,8,8,1024]{3,2,0,1:T(8,128)(2,1)} copy(bf16[16,8,8,1024]{3,2,1,0:T(8,128)(2,1)S(1)} %bitcast.28) | data formatting | bytes 4194304 | tf_op jit(solution)/shard_map/reshape | solution.py:328
  8.8 6.9 %all-to-all-done.1.refs_2_.refs_4_ = bf16[8,256,128]{2,1,0:T(8,128)(2,1)S(1)} async-done(((bf16[8,256,128]{2,1,0:T(8,128)(2,1)}), bf16[8,256,128]{2,1,0:T(8,128)(2,1)S(1)}, u32[]{:S(2)}, u32[]{:S(2)}) %all-to-all-start.1) | async-done | bytes 524320 | tf_op jit(solution)/shard_map/all_to_all | solution.py:316
  15.7 0.0 copy-start.3
  15.7 4.5 %all-to-all-start = ((bf16[8,128,1024]{2,1,0:T(8,128)(2,1)}), bf16[8,128,1024]{2,1,0:T(8,128)(2,1)S(1)}, u32[]{:S(2)}, u32[]{:S(2)}) async-start(bf16[8,128,1024]{2,1,0:T(8,128)(2,1)} %bitcast.27), calls=%async_computation | async-start | bytes 4194304 | tf_op jit(solution)/shard_map/all_to_all | solution.py:329
  20.1 1.3 %collective-permute-start = (bf16[8,256,128]{2,1,0:T(8,128)(2,1)S(1)}, bf16[8,256,128]{2,1,0:T(8,128)(2,1)S(1)}, u32[]{:S(2)}, u32[]{:S(2)}) collective-permute-start(bf16[8,256,128]{2,1,0:T(8,128)(2,1)S(1)} %all-to-all-done.1.refs_2_.refs_4_), channel_id=1, source_target_pairs={{0,8},{8,16},{16,24},{24,0},{1,9},{9,17},{17,25},{25,1},{2,10},{10... | collective-permute-start | bytes 1572872 | tf_op jit(solution)/shard_map/ppermute | solution.py:331
  21.4 0.2 collective-permute-start.1
  21.6 0.1 stack.53
  21.7 0.0 copy-done.3
  21.7 0.2 convert_reduce_fusion
  21.9 0.1 select_reduce_fusion
  22.0 0.1 concatenate.3.refs_0_
  22.1 11.5 %collective-permute-done.refs_3_.refs_5_ = bf16[8,256,128]{2,1,0:T(8,128)(2,1)S(1)} collective-permute-done((bf16[8,256,128]{2,1,0:T(8,128)(2,1)S(1)}, bf16[8,256,128]{2,1,0:T(8,128)(2,1)S(1)}, u32[]{:S(2)}, u32[]{:S(2)}) %collective-permute-start) | collective-permute-done | bytes 524320 | tf_op jit(solution)/shard_map/ppermute | solution.py:331
  33.6 3.3 %collective-permute-start.2 = (bf16[8,256,128]{2,1,0:T(8,128)(2,1)S(1)}, bf16[8,256,128]{2,1,0:T(8,128)(2,1)}, u32[]{:S(2)}, u32[]{:S(2)}) collective-permute-start(bf16[8,256,128]{2,1,0:T(8,128)(2,1)S(1)} %collective-permute-done.refs_3_.refs_5_), channel_id=1, source_target_pairs={{8,16},{16,24},{9,17},{17,25},{10,18},{18,26},{11,19},{19,27},{12,... | collective-permute-start | bytes 1572872 | tf_op jit(solution)/shard_map/ppermute | solution.py:333
  36.9 7.9 %collective-permute-done.1.refs_4_.refs_6_ = bf16[8,256,128]{2,1,0:T(8,128)(2,1)} collective-permute-done((bf16[8,256,128]{2,1,0:T(8,128)(2,1)S(1)}, bf16[8,256,128]{2,1,0:T(8,128)(2,1)}, u32[]{:S(2)}, u32[]{:S(2)}) %collective-permute-start.1) | collective-permute-done | bytes 524320 | tf_op jit(solution)/shard_map/ppermute | solution.py:332
  44.8 4.3 %collective-permute-start.3 = (bf16[8,256,128]{2,1,0:T(8,128)(2,1)}, bf16[8,256,128]{2,1,0:T(8,128)(2,1)}, u32[]{:S(2)}, u32[]{:S(2)}) collective-permute-start(bf16[8,256,128]{2,1,0:T(8,128)(2,1)} %collective-permute-done.1.refs_4_.refs_6_), channel_id=1, source_target_pairs={{8,0},{16,8},{9,1},{17,9},{10,2},{18,10},{11,3},{19,11},{12,4},{20... | collective-permute-start | bytes 1572872 | tf_op jit(solution)/shard_map/ppermute | solution.py:334
  49.1 0.0 all-to-all-done
  49.1 19.2 %near.1 = (f32[8,144,1024]{2,1,0:T(8,128)S(1)}, f32[8,8,1024]{2,1,0:T(8,128)S(1)}) custom-call(s32[184]{0:T(256)S(1)} %concatenate.3.refs_0_, bf16[1024,1024]{1,0:T(8,128)(2,1)S(1)} %bitcast.23, bf16[8,256,128]{2,1,0:T(8,128)(2,1)S(1)} %all-to-all-done.1.refs_2_.refs_4_, bf16[8,256,128]{2,1,0:T(8,128)(2,1)S(1)} %collective-permute-done.refs_3_.refs_5_, ...), custom_call_target="tpu_custom_call" | custom-call | flops 12884901888 | bytes 6291456 | tf_op jit(solution)/shard_map/near/pallas_call | solution.py:209
  68.3 0.0 collective-permute-done.2.refs_7_
  68.3 0.0 collective-permute-done.3.refs_8_
  68.3 3.4 %far.5 = (bf16[128,1024]{1,0:T(8,128)(2,1)S(1)}, bf16[128,1024]{1,0:T(8,128)(2,1)S(1)}) custom-call(s32[184]{0:T(256)S(1)} %concatenate.3.refs_0_, bf16[1024,1024]{1,0:T(8,128)(2,1)S(1)} %bitcast.24, f32[8,144,1024]{2,1,0:T(8,128)S(1)} %get-tuple-element.15.refs_2_, f32[8,8,1024]{2,1,0:T(8,128)S(1)} %get-tuple-element.16.refs_3_, ...), custom_call_target="tpu_custom_call" | custom-call | flops 1073741824 | bytes 6291456 | tf_op jit(solution)/shard_map/far/pallas_call | solution.py:246
  71.7 6.9 %collective-permute-start.10 = (bf16[128,1024]{1,0:T(8,128)(2,1)S(1)}, bf16[128,1024]{1,0:T(8,128)(2,1)S(1)}, u32[]{:S(2)}, u32[]{:S(2)}) collective-permute-start(bf16[128,1024]{1,0:T(8,128)(2,1)S(1)} %get-tuple-element.24), channel_id=1, source_target_pairs={{0,7},{1,6},{2,5},{3,4},{4,3},{5,2},{6,1},{7,0},{8,15},{9,14},{10,... | collective-permute-start | bytes 786440 | tf_op jit(solution)/shard_map/ppermute | solution.py:283
  78.6 0.0 collective-permute-start.8
  78.6 5.3 %far.4 = (bf16[128,1024]{1,0:T(8,128)(2,1)S(1)}, bf16[128,1024]{1,0:T(8,128)(2,1)S(1)}, bf16[128,1024]{1,0:T(8,128)(2,1)S(1)}) custom-call(s32[184]{0:T(256)S(1)} %concatenate.3.refs_0_, bf16[1024,1024]{1,0:T(8,128)(2,1)S(1)} %bitcast.25, f32[8,144,1024]{2,1,0:T(8,128)S(1)} %get-tuple-element.15.refs_2_, f32[8,8,1024]{2,1,0:T(8,128)S(1)} %get-tuple-element.16.refs_3_, ...), custom_call_target="tpu_custom_call" | custom-call | flops 1610612736 | bytes 6291456 | tf_op jit(solution)/shard_map/far/pallas_call | solution.py:246
  83.9 1.0 %collective-permute-start.4 = (bf16[128,1024]{1,0:T(8,128)(2,1)S(1)}, bf16[128,1024]{1,0:T(8,128)(2,1)S(1)}, u32[]{:S(2)}, u32[]{:S(2)}) collective-permute-start(bf16[128,1024]{1,0:T(8,128)(2,1)S(1)} %get-tuple-element.18), channel_id=1, source_target_pairs={{0,1},{1,0},{2,3},{3,2},{4,5},{5,4},{6,7},{7,6},{8,9},{9,8},{10,11... | collective-permute-start | bytes 786440 | tf_op jit(solution)/shard_map/ppermute | solution.py:283
  84.9 0.7 collective-permute-start.6
  85.6 0.5 collective-permute-start.7
  86.1 4.9 %far.3 = (bf16[128,1024]{1,0:T(8,128)(2,1)S(1)}, bf16[128,1024]{1,0:T(8,128)(2,1)S(1)}, bf16[128,1024]{1,0:T(8,128)(2,1)S(1)}) custom-call(s32[184]{0:T(256)S(1)} %concatenate.3.refs_0_, bf16[1024,1024]{1,0:T(8,128)(2,1)S(1)} %bitcast.26, f32[8,144,1024]{2,1,0:T(8,128)S(1)} %get-tuple-element.15.refs_2_, f32[8,8,1024]{2,1,0:T(8,128)S(1)} %get-tuple-element.16.refs_3_, ...), custom_call_target="tpu_custom_call" | custom-call | flops 1610612736 | bytes 6291456 | tf_op jit(solution)/shard_map/far/pallas_call | solution.py:246
  91.1 0.0 collective-permute-done.10.refs_7_
  91.1 1.2 %collective-permute-start.5 = (bf16[128,1024]{1,0:T(8,128)(2,1)S(1)}, bf16[128,1024]{1,0:T(8,128)(2,1)S(1)}, u32[]{:S(2)}, u32[]{:S(2)}) collective-permute-start(bf16[128,1024]{1,0:T(8,128)(2,1)S(1)} %get-tuple-element.19), channel_id=1, source_target_pairs={{0,2},{1,3},{2,0},{3,1},{4,6},{5,7},{6,4},{7,5},{8,10},{9,11},{10,... | collective-permute-start | bytes 786440 | tf_op jit(solution)/shard_map/ppermute | solution.py:283
  92.3 0.0 collective-permute-done.8.refs_5_
  92.3 0.7 collective-permute-start.9
  93.0 4.0 %collective-permute-done.4.refs_1_ = bf16[128,1024]{1,0:T(8,128)(2,1)S(1)} collective-permute-done((bf16[128,1024]{1,0:T(8,128)(2,1)S(1)}, bf16[128,1024]{1,0:T(8,128)(2,1)S(1)}, u32[]{:S(2)}, u32[]{:S(2)}) %collective-permute-start.4) | collective-permute-done | bytes 262176 | tf_op jit(solution)/shard_map/ppermute | solution.py:283
  97.0 4.0 %collective-permute-done.6.refs_3_ = bf16[128,1024]{1,0:T(8,128)(2,1)S(1)} collective-permute-done((bf16[128,1024]{1,0:T(8,128)(2,1)S(1)}, bf16[128,1024]{1,0:T(8,128)(2,1)S(1)}, u32[]{:S(2)}, u32[]{:S(2)}) %collective-permute-start.6) | collective-permute-done | bytes 262176 | tf_op jit(solution)/shard_map/ppermute | solution.py:283
  101.0 0.0 collective-permute-done.7.refs_4_
  101.0 0.0 collective-permute-done.5.refs_2_
  101.0 0.8 collective-permute-done.9.refs_6_
  101.8 1.5 %unpack.1 = bf16[128,8192]{1,0:T(8,128)(2,1)} custom-call(s32[1]{0:T(128)} %bitcast.me_ref, bf16[128,1024]{1,0:T(8,128)(2,1)S(1)} %get-tuple-element.17.refs_0_, bf16[128,1024]{1,0:T(8,128)(2,1)S(1)} %collective-permute-done.4.refs_1_, bf16[128,1024]{1,0:T(8,128)(2,1)S(1)} %collective-permute-done.5.refs_2_, ...), custom_call_target="tpu_custom_call" | custom-call | tf_op jit(solution)/shard_map/unpack/pallas_call | solution.py:286
  (2 shorter events, 0.0 us)
Async XLA Ops:
  0.0 0.9 copy-start
  1.0 0.9 copy-start.1
  1.9 5.3 %copy-start.2 = (bf16[128,8192]{1,0:T(8,128)(2,1)S(1)}, bf16[128,8192]{1,0:T(8,128)(2,1)}, u32[]{:S(2)}) copy-start(bf16[128,8192]{1,0:T(8,128)(2,1)} %param.4) | copy-start | bytes 6291460
  2.8 12.8 %all-to-all-start.1 = ((bf16[8,256,128]{2,1,0:T(8,128)(2,1)}), bf16[8,256,128]{2,1,0:T(8,128)(2,1)S(1)}, u32[]{:S(2)}, u32[]{:S(2)}) async-start(bf16[8,256,128]{2,1,0:T(8,128)(2,1)} %pack.1), calls=%async_computation.1 | async-start | bytes 1048576 | tf_op jit(solution)/shard_map/all_to_all | solution.py:316
  15.7 6.0 %copy-start.3 = (s32[32]{0:T(128)S(1)}, s32[32]{0:T(128)}, u32[]{:S(2)}) copy-start(s32[32]{0:T(128)} %param.7) | copy-start | bytes 388
  15.7 33.4 %all-to-all-start = ((bf16[8,128,1024]{2,1,0:T(8,128)(2,1)}), bf16[8,128,1024]{2,1,0:T(8,128)(2,1)S(1)}, u32[]{:S(2)}, u32[]{:S(2)}) async-start(bf16[8,128,1024]{2,1,0:T(8,128)(2,1)} %bitcast.27), calls=%async_computation | async-start | bytes 4194304 | tf_op jit(solution)/shard_map/all_to_all | solution.py:329
  20.1 13.5 %collective-permute-start = (bf16[8,256,128]{2,1,0:T(8,128)(2,1)S(1)}, bf16[8,256,128]{2,1,0:T(8,128)(2,1)S(1)}, u32[]{:S(2)}, u32[]{:S(2)}) collective-permute-start(bf16[8,256,128]{2,1,0:T(8,128)(2,1)S(1)} %all-to-all-done.1.refs_2_.refs_4_), channel_id=1, source_target_pairs={{0,8},{8,16},{16,24},{24,0},{1,9},{9,17},{17,25},{25,1},{2,10},{10... | collective-permute-start | bytes 1572872 | tf_op jit(solution)/shard_map/ppermute | solution.py:331
  21.4 23.4 %collective-permute-start.1 = (bf16[8,256,128]{2,1,0:T(8,128)(2,1)S(1)}, bf16[8,256,128]{2,1,0:T(8,128)(2,1)}, u32[]{:S(2)}, u32[]{:S(2)}) collective-permute-start(bf16[8,256,128]{2,1,0:T(8,128)(2,1)S(1)} %all-to-all-done.1.refs_2_.refs_4_), channel_id=1, source_target_pairs={{0,24},{8,0},{16,8},{24,16},{1,25},{9,1},{17,9},{25,17},{2,26},{10... | collective-permute-start | bytes 1572872 | tf_op jit(solution)/shard_map/ppermute | solution.py:332
  33.6 34.7 %collective-permute-start.2 = (bf16[8,256,128]{2,1,0:T(8,128)(2,1)S(1)}, bf16[8,256,128]{2,1,0:T(8,128)(2,1)}, u32[]{:S(2)}, u32[]{:S(2)}) collective-permute-start(bf16[8,256,128]{2,1,0:T(8,128)(2,1)S(1)} %collective-permute-done.refs_3_.refs_5_), channel_id=1, source_target_pairs={{8,16},{16,24},{9,17},{17,25},{10,18},{18,26},{11,19},{19,27},{12,... | collective-permute-start | bytes 1572872 | tf_op jit(solution)/shard_map/ppermute | solution.py:333
  44.8 23.5 %collective-permute-start.3 = (bf16[8,256,128]{2,1,0:T(8,128)(2,1)}, bf16[8,256,128]{2,1,0:T(8,128)(2,1)}, u32[]{:S(2)}, u32[]{:S(2)}) collective-permute-start(bf16[8,256,128]{2,1,0:T(8,128)(2,1)} %collective-permute-done.1.refs_4_.refs_6_), channel_id=1, source_target_pairs={{8,0},{16,8},{9,1},{17,9},{10,2},{18,10},{11,3},{19,11},{12,4},{20... | collective-permute-start | bytes 1572872 | tf_op jit(solution)/shard_map/ppermute | solution.py:334
  71.7 19.4 %collective-permute-start.10 = (bf16[128,1024]{1,0:T(8,128)(2,1)S(1)}, bf16[128,1024]{1,0:T(8,128)(2,1)S(1)}, u32[]{:S(2)}, u32[]{:S(2)}) collective-permute-start(bf16[128,1024]{1,0:T(8,128)(2,1)S(1)} %get-tuple-element.24), channel_id=1, source_target_pairs={{0,7},{1,6},{2,5},{3,4},{4,3},{5,2},{6,1},{7,0},{8,15},{9,14},{10,... | collective-permute-start | bytes 786440 | tf_op jit(solution)/shard_map/ppermute | solution.py:283
  78.6 13.7 %collective-permute-start.8 = (bf16[128,1024]{1,0:T(8,128)(2,1)S(1)}, bf16[128,1024]{1,0:T(8,128)(2,1)S(1)}, u32[]{:S(2)}, u32[]{:S(2)}) collective-permute-start(bf16[128,1024]{1,0:T(8,128)(2,1)S(1)} %get-tuple-element.22), channel_id=1, source_target_pairs={{0,5},{1,4},{2,7},{3,6},{4,1},{5,0},{6,3},{7,2},{8,13},{9,12},{10,... | collective-permute-start | bytes 786440 | tf_op jit(solution)/shard_map/ppermute | solution.py:283
  83.9 13.1 %collective-permute-start.4 = (bf16[128,1024]{1,0:T(8,128)(2,1)S(1)}, bf16[128,1024]{1,0:T(8,128)(2,1)S(1)}, u32[]{:S(2)}, u32[]{:S(2)}) collective-permute-start(bf16[128,1024]{1,0:T(8,128)(2,1)S(1)} %get-tuple-element.18), channel_id=1, source_target_pairs={{0,1},{1,0},{2,3},{3,2},{4,5},{5,4},{6,7},{7,6},{8,9},{9,8},{10,11... | collective-permute-start | bytes 786440 | tf_op jit(solution)/shard_map/ppermute | solution.py:283
  84.9 16.1 %collective-permute-start.6 = (bf16[128,1024]{1,0:T(8,128)(2,1)S(1)}, bf16[128,1024]{1,0:T(8,128)(2,1)S(1)}, u32[]{:S(2)}, u32[]{:S(2)}) collective-permute-start(bf16[128,1024]{1,0:T(8,128)(2,1)S(1)} %get-tuple-element.20), channel_id=1, source_target_pairs={{0,3},{1,2},{2,1},{3,0},{4,7},{5,6},{6,5},{7,4},{8,11},{9,10},{10,... | collective-permute-start | bytes 786440 | tf_op jit(solution)/shard_map/ppermute | solution.py:283
  85.6 15.4 %collective-permute-start.7 = (bf16[128,1024]{1,0:T(8,128)(2,1)S(1)}, bf16[128,1024]{1,0:T(8,128)(2,1)S(1)}, u32[]{:S(2)}, u32[]{:S(2)}) collective-permute-start(bf16[128,1024]{1,0:T(8,128)(2,1)S(1)} %get-tuple-element.21), channel_id=1, source_target_pairs={{0,4},{1,5},{2,6},{3,7},{4,0},{5,1},{6,2},{7,3},{8,12},{9,13},{10,... | collective-permute-start | bytes 786440 | tf_op jit(solution)/shard_map/ppermute | solution.py:283
  91.1 9.9 %collective-permute-start.5 = (bf16[128,1024]{1,0:T(8,128)(2,1)S(1)}, bf16[128,1024]{1,0:T(8,128)(2,1)S(1)}, u32[]{:S(2)}, u32[]{:S(2)}) collective-permute-start(bf16[128,1024]{1,0:T(8,128)(2,1)S(1)} %get-tuple-element.19), channel_id=1, source_target_pairs={{0,2},{1,3},{2,0},{3,1},{4,6},{5,7},{6,4},{7,5},{8,10},{9,11},{10,... | collective-permute-start | bytes 786440 | tf_op jit(solution)/shard_map/ppermute | solution.py:283
  92.3 9.5 %collective-permute-start.9 = (bf16[128,1024]{1,0:T(8,128)(2,1)S(1)}, bf16[128,1024]{1,0:T(8,128)(2,1)S(1)}, u32[]{:S(2)}, u32[]{:S(2)}) collective-permute-start(bf16[128,1024]{1,0:T(8,128)(2,1)S(1)} %get-tuple-element.23), channel_id=1, source_target_pairs={{0,6},{1,7},{2,4},{3,5},{4,2},{5,3},{6,0},{7,1},{8,14},{9,15},{10,... | collective-permute-start | bytes 786440 | tf_op jit(solution)/shard_map/ppermute | solution.py:283

commit v3 on v2

--- a/solution.py
+++ b/solution.py
@@ -21,7 +21,7 @@
 VMEM = 24 * 2**20
 NT = (((1,), (1,)), ((), ()))
 GROUP_AXES = ("inner", "head")
-PARTS = ((5, 7), (1, 4, 3), (6, 2, 0))
+PARTS = (((5, 7), (1, 4, 3, 6)), ((2, 0),))
 
 
 def queries_of(q_ref):
@@ -68,7 +68,7 @@
         self.sequence = 16 + spans * 5
 
 
-def near_kernel(at, n_kv, *refs):
+def near_kernel(at, offset, n_kv, *refs):
     t_ref, q_ref = refs[:2]
     pieces = refs[2 : 2 + n_kv]
     acc_ref, m_ref, kv_ref, sems = refs[2 + n_kv :]
@@ -87,15 +87,15 @@
         for copy in copies:
             copy.wait()
 
-    rank = t_ref[at.near_rank + t_ref[at.first] + step]
+    rank = t_ref[at.near_rank + t_ref[at.first] + t_ref[at.sequence + offset + step]]
 
     def first_block(count):
-        start = at.near_list + rank + 1 - count
-        keys, values = gather(kv_ref, [t_ref[start + t] for t in range(count)])
+        others = [t_ref[at.near_list + rank - t] for t in range(1, count)]
+        keys, values = gather(kv_ref, [t_ref[at.near_list + rank], *others])
         s = scores(keys, q_ref)
-        own = causal(s[(count - 1) * SPAN :])
-        s = jnp.concatenate([s[: (count - 1) * SPAN], own], 0) if count > 1 else own
-        m = jnp.max(s, axis=0, keepdims=True)
+        own = causal(s[:SPAN])
+        m = jnp.max(own, axis=0, keepdims=True)
+        s = jnp.concatenate([own, s[SPAN:]], 0) if count > 1 else own
         m_ref[0] = jnp.broadcast_to(m, m_ref.shape[1:])
         acc_ref[0] = blend(values, jnp.exp2(s - m))
 
@@ -206,37 +206,41 @@
             transcendentals=int(elements * part),
         )
 
-    acc, m = pl.pallas_call(
-        functools.partial(near_kernel, at, len(near)),
-        grid_spec=pltpu.PrefetchScalarGridSpec(
-            num_scalar_prefetch=1,
-            grid=(q_spans,),
-            in_specs=[pl.BlockSpec((SPAN, GROUP * HD), lambda i, t: (i, 0))] + [anywhere] * len(near),
-            out_specs=[
-                pl.BlockSpec((1, HD + EXTRA, ROWS), lambda i, t: (i, 0, 0)),
-                pl.BlockSpec((1, 8, ROWS), lambda i, t: (i, 0, 0)),
+    def begin(offset, count, q):
+        return pl.pallas_call(
+            functools.partial(near_kernel, at, offset, len(near)),
+            grid_spec=pltpu.PrefetchScalarGridSpec(
+                num_scalar_prefetch=1,
+                grid=(count,),
+                in_specs=[pl.BlockSpec((SPAN, GROUP * HD), lambda i, t: (t[at.sequence + offset + i], 0))]
+                + [anywhere] * len(near),
+                out_specs=[
+                    pl.BlockSpec((1, HD + EXTRA, ROWS), lambda i, t: (i, 0, 0)),
+                    pl.BlockSpec((1, 8, ROWS), lambda i, t: (i, 0, 0)),
+                ],
+                scratch_shapes=[
+                    pltpu.VMEM((spans, SPAN + HD, SPAN), jnp.bfloat16),
+                    pltpu.SemaphoreType.DMA((len(near),)),
+                ],
+            ),
+            out_shape=[
+                jax.ShapeDtypeStruct((count, HD + EXTRA, ROWS), jnp.float32),
+                jax.ShapeDtypeStruct((count, 8, ROWS), jnp.float32),
             ],
-            scratch_shapes=[
-                pltpu.VMEM((spans, SPAN + HD, SPAN), jnp.bfloat16),
-                pltpu.SemaphoreType.DMA((len(near),)),
-            ],
-        ),
-        out_shape=[
-            jax.ShapeDtypeStruct((q_spans, HD + EXTRA, ROWS), jnp.float32),
-            jax.ShapeDtypeStruct((q_spans, 8, ROWS), jnp.float32),
-        ],
-        compiler_params=limit,
-        cost_estimate=cost(0.75),
-        name="near",
-    )(table, q, *near)
-
-    def finish(offset, count, apart):
+            compiler_params=limit,
+            cost_estimate=cost(0.75 * count / q_spans),
+            name="near",
+        )(table, q, *near)
+
+    def finish(begun, begun_at, offset, count, apart):
+        skip = offset - begun_at
+
         def nth(i, t):
             return t[at.sequence + offset + i]
 
         q_block = pl.BlockSpec((SPAN, GROUP * HD), lambda i, t: (nth(i, t), 0))
-        acc_block = pl.BlockSpec((1, HD + EXTRA, ROWS), lambda i, t: (nth(i, t), 0, 0))
-        m_block = pl.BlockSpec((1, 8, ROWS), lambda i, t: (nth(i, t), 0, 0))
+        acc_block = pl.BlockSpec((1, HD + EXTRA, ROWS), lambda i, t: (skip + i, 0, 0))
+        m_block = pl.BlockSpec((1, 8, ROWS), lambda i, t: (skip + i, 0, 0))
         if apart:
             out_specs = [pl.BlockSpec((SPAN, GROUP * HD), lambda i, t: (0, 0))] * count
             out_shape = [jax.ShapeDtypeStruct((SPAN, GROUP * HD), q.dtype)] * count
@@ -262,9 +266,9 @@
             compiler_params=limit,
             cost_estimate=cost(0.25 * count / q_spans),
             name="far",
-        )(table, q, acc, m, *near, *far)
-
-    return finish
+        )(table, q, *begun, *near, *far)
+
+    return begin, finish
 
 
 def unpack_kernel(me_ref, *refs):
@@ -274,15 +278,21 @@
         o_ref[:, pl.ds(column, GROUP * HD)] = part_ref[...]
 
 
-def to_token_owners(finish, me):
+def to_token_owners(q, begin, finish, me):
     parts = [None] * KVH
     offset = 0
-    for steps in PARTS:
-        for step, done in zip(steps, finish(offset, len(steps), True)):
-            if step:
-                done = lax.ppermute(done, GROUP_AXES, [(i, i ^ step) for i in range(KVH)])
-            parts[step] = done
-        offset += len(steps)
+    for together in PARTS:
+        begun_at = offset
+        begun = begin(offset, sum(map(len, together)), q)
+        for steps in together:
+            finished = finish(begun, begun_at, offset, len(steps), True)
+            offset += len(steps)
+            for step, done in zip(steps, finished):
+                if step:
+                    parts[step] = lax.ppermute(done, GROUP_AXES, [(i, i ^ step) for i in range(KVH)])
+                else:
+                    parts[step] = done
+        q, _ = lax.optimization_barrier((q, (finished, [parts[step] for step in together[0]])))
     return pl.pallas_call(
         unpack_kernel,
         grid_spec=pltpu.PrefetchScalarGridSpec(
@@ -310,8 +320,7 @@
     )
     if rows == SPAN:
         packed = pl.pallas_call(
-            pack_kernel, out_shape=jax.ShapeDtypeStruct((KVH, SPAN + HD, SPAN), key_rows.dtype), name="pack",
-            compiler_params=pltpu.CompilerParams(vmem_limit_bytes=VMEM),
+            pack_kernel, out_shape=jax.ShapeDtypeStruct((KVH, SPAN + HD, SPAN), key_rows.dtype), name="pack"
         )(key_rows, value_rows)
         return exchange(packed)
     packed = jnp.concatenate([key_rows.reshape(rows, KVH, HD), value_rows.reshape(rows, KVH, HD)], 2)
@@ -343,13 +352,13 @@
         far, far_bases, far_first = [], [], jnp.int32(0)
     me = lax.axis_index(GROUP_AXES).astype(jnp.int32)
     if rows == SPAN:
-        sequence = jnp.stack([me ^ step for steps in PARTS for step in steps])
+        sequence = jnp.stack([me ^ step for together in PARTS for steps in together for step in steps])
     else:
         sequence = jnp.arange(group_spans, dtype=jnp.int32)
-    finish = attention(q, near, far, near_bases, far_bases, far_first, place * group_spans, span_order, sequence)
+    begin, finish = attention(q, near, far, near_bases, far_bases, far_first, place * group_spans, span_order, sequence)
     if rows == SPAN:
-        return to_token_owners(finish, me)
-    out = finish(0, group_spans, False)[0]
+        return to_token_owners(q, begin, finish, me)
+    out = finish(begin(0, group_spans, q), 0, 0, group_spans, False)[0]
     out = lax.all_to_all(out.reshape(KVH, rows, GROUP * HD), GROUP_AXES, split_axis=0, concat_axis=0, tiled=False)
     return out.transpose(1, 0, 2).reshape(rows, HQ * HD)
 

time: 104 us -> 98.1 us (0.943)
  the two profiles are of different devices: /device:TPU:17 before, /device:TPU:11 now
where the time goes in v3:
time: 98.1 us; the launch traced here: 99.7 us
  Pallas kernels  35.9 us (37%)
  starting transfers between devices  32.7 us (33%)
  waiting for transfers between devices  28.9 us (29%)
  local copies, waits for them, and re-layouts  1.75 us (2%)
    pallas_call x2, Pallas kernels, begin(): pl.pallas_call(functools.partial(near_kernel, at, offset, len(near)), gri...  20.3 us
    ppermute x7, starting transfers between devices, to_token_owners(): lax.ppermute(done, GROUP_AXES, [(i, i ^ step) for i in range(KVH)])  15.5 us
    pallas_call x3, Pallas kernels, finish(): pl.pallas_call(functools.partial(far_kernel, at, offset, n_kv, len(far),...  12.1 us
    ppermute x1, waiting for transfers between devices, shards(): lax.ppermute(own, 'outer', [(i, (i + 1) % outer) for i in range(outer)])  11.2 us
    ppermute x1, waiting for transfers between devices, shards(): lax.ppermute(own, 'outer', [(i, (i - 1) % outer) for i in range(outer)])  8.79 us
    all_to_all x1, waiting for transfers between devices, to_head_owners(): return exchange(packed)  6.21 us
    all_to_all x1, starting transfers between devices, shards(): lax.all_to_all(q, GROUP_AXES, split_axis=0, concat_axis=0, tiled=False)  5.13 us
    all_to_all x1, starting transfers between devices, to_head_owners(): return exchange(packed)  4.57 us
  transfers between devices with their start and end apart: 13, of which 5 were waited for; matrix products, arithmetic and copies ran while one was open for 2% of the time, Pallas kernels for 29%

profile of v3, /device:TPU:11, one launch (start us, length us, event | category | flops | bytes accessed | tf_op | source)
XLA Modules:
  0.0 99.7 jit_solution(10875859834403676201)
XLA Ops:
  0.0 0.0 copy-start
  0.0 2.1 %pack.1 = bf16[8,256,128]{2,1,0:T(8,128)(2,1)} custom-call(bf16[128,1024]{1,0:T(8,128)(2,1)} %k_ref.1, bf16[128,1024]{1,0:T(8,128)(2,1)} %v_ref.1), custom_call_target="tpu_custom_call" | custom-call | tf_op jit(solution)/shard_map/pack/pallas_call | solution.py:322
  2.1 4.6 %all-to-all-start.1 = ((bf16[8,256,128]{2,1,0:T(8,128)(2,1)}), bf16[8,256,128]{2,1,0:T(8,128)(2,1)S(1)}, u32[]{:S(2)}, u32[]{:S(2)}) async-start(bf16[8,256,128]{2,1,0:T(8,128)(2,1)} %pack.1), calls=%async_computation.1 | async-start | bytes 1048576 | tf_op jit(solution)/shard_map/all_to_all | solution.py:325
  6.7 0.0 copy-done
  6.7 1.6 %copy.9 = bf16[16,8,8,1024]{3,2,0,1:T(8,128)(2,1)} copy(bf16[16,8,8,1024]{3,2,1,0:T(8,128)(2,1)S(1)} %bitcast.29) | data formatting | bytes 4194304 | tf_op jit(solution)/shard_map/reshape | solution.py:337
  8.2 6.2 %all-to-all-done.1.refs_2_.refs_4_ = bf16[8,256,128]{2,1,0:T(8,128)(2,1)S(1)} async-done(((bf16[8,256,128]{2,1,0:T(8,128)(2,1)}), bf16[8,256,128]{2,1,0:T(8,128)(2,1)S(1)}, u32[]{:S(2)}, u32[]{:S(2)}) %all-to-all-start.1) | async-done | bytes 524320 | tf_op jit(solution)/shard_map/all_to_all | solution.py:325
  14.4 0.0 copy-start.1
  14.4 5.1 %all-to-all-start = ((bf16[8,128,1024]{2,1,0:T(8,128)(2,1)}), bf16[8,128,1024]{2,1,0:T(8,128)(2,1)S(1)}, u32[]{:S(2)}, u32[]{:S(2)}) async-start(bf16[8,128,1024]{2,1,0:T(8,128)(2,1)} %bitcast.28), calls=%async_computation | async-start | bytes 4194304 | tf_op jit(solution)/shard_map/all_to_all | solution.py:338
  19.6 1.3 %collective-permute-start = (bf16[8,256,128]{2,1,0:T(8,128)(2,1)S(1)}, bf16[8,256,128]{2,1,0:T(8,128)(2,1)S(1)}, u32[]{:S(2)}, u32[]{:S(2)}) collective-permute-start(bf16[8,256,128]{2,1,0:T(8,128)(2,1)S(1)} %all-to-all-done.1.refs_2_.refs_4_), channel_id=1, source_target_pairs={{0,8},{8,16},{16,24},{24,0},{1,9},{9,17},{17,25},{25,1},{2,10},{10... | collective-permute-start | bytes 1572872 | tf_op jit(solution)/shard_map/ppermute | solution.py:340
  20.9 0.2 collective-permute-start.1
  21.0 0.1 stack.53
  21.1 0.0 copy-done.1
  21.2 0.2 convert_reduce_fusion
  21.3 0.1 select_reduce_fusion
  21.5 0.1 concatenate.3.refs_0_
  21.6 11.2 %collective-permute-done.refs_3_.refs_5_ = bf16[8,256,128]{2,1,0:T(8,128)(2,1)S(1)} collective-permute-done((bf16[8,256,128]{2,1,0:T(8,128)(2,1)S(1)}, bf16[8,256,128]{2,1,0:T(8,128)(2,1)S(1)}, u32[]{:S(2)}, u32[]{:S(2)}) %collective-permute-start) | collective-permute-done | bytes 524320 | tf_op jit(solution)/shard_map/ppermute | solution.py:340
  32.7 4.1 %collective-permute-start.2 = (bf16[8,256,128]{2,1,0:T(8,128)(2,1)S(1)}, bf16[8,256,128]{2,1,0:T(8,128)(2,1)}, u32[]{:S(2)}, u32[]{:S(2)}) collective-permute-start(bf16[8,256,128]{2,1,0:T(8,128)(2,1)S(1)} %collective-permute-done.refs_3_.refs_5_), channel_id=1, source_target_pairs={{8,16},{16,24},{9,17},{17,25},{10,18},{18,26},{11,19},{19,27},{12,... | collective-permute-start | bytes 1572872 | tf_op jit(solution)/shard_map/ppermute | solution.py:342
  36.8 8.8 %collective-permute-done.1.refs_4_.refs_6_ = bf16[8,256,128]{2,1,0:T(8,128)(2,1)} collective-permute-done((bf16[8,256,128]{2,1,0:T(8,128)(2,1)S(1)}, bf16[8,256,128]{2,1,0:T(8,128)(2,1)}, u32[]{:S(2)}, u32[]{:S(2)}) %collective-permute-start.1) | collective-permute-done | bytes 524320 | tf_op jit(solution)/shard_map/ppermute | solution.py:341
  45.6 1.9 %collective-permute-start.3 = (bf16[8,256,128]{2,1,0:T(8,128)(2,1)}, bf16[8,256,128]{2,1,0:T(8,128)(2,1)}, u32[]{:S(2)}, u32[]{:S(2)}) collective-permute-start(bf16[8,256,128]{2,1,0:T(8,128)(2,1)} %collective-permute-done.1.refs_4_.refs_6_), channel_id=1, source_target_pairs={{8,0},{16,8},{9,1},{17,9},{10,2},{18,10},{11,3},{19,11},{12,4},{20... | collective-permute-start | bytes 1572872 | tf_op jit(solution)/shard_map/ppermute | solution.py:343
  47.6 0.0 all-to-all-done
  47.6 12.5 %near.2 = (f32[6,144,1024]{2,1,0:T(8,128)S(1)}, f32[6,8,1024]{2,1,0:T(8,128)S(1)}) custom-call(s32[184]{0:T(256)S(1)} %concatenate.3.refs_0_, bf16[1024,1024]{1,0:T(8,128)(2,1)S(1)} %bitcast.23, bf16[8,256,128]{2,1,0:T(8,128)(2,1)S(1)} %all-to-all-done.1.refs_2_.refs_4_, bf16[8,256,128]{2,1,0:T(8,128)(2,1)S(1)} %collective-permute-done.refs_3_.refs_5_, ...), custom_call_target="tpu_custom_call" | custom-call | flops 9663676416 | bytes 6291456 | tf_op jit(solution)/shard_map/near/pallas_call | solution.py:210
  60.0 0.0 collective-permute-done.2.refs_7_
  60.0 0.0 collective-permute-done.3.refs_8_
  60.1 3.0 %far.4 = (bf16[128,1024]{1,0:T(8,128)(2,1)S(1)}, bf16[128,1024]{1,0:T(8,128)(2,1)S(1)}) custom-call(s32[184]{0:T(256)S(1)} %concatenate.3.refs_0_, bf16[1024,1024]{1,0:T(8,128)(2,1)S(1)} %bitcast.24, f32[6,144,1024]{2,1,0:T(8,128)S(1)} %get-tuple-element.18.refs_2_, f32[6,8,1024]{2,1,0:T(8,128)S(1)} %get-tuple-element.19.refs_3_, ...), custom_call_target="tpu_custom_call" | custom-call | flops 1073741824 | bytes 6291456 | tf_op jit(solution)/shard_map/far/pallas_call | solution.py:250
  63.0 5.7 %collective-permute-start.4 = (bf16[128,1024]{1,0:T(8,128)(2,1)S(1)}, bf16[128,1024]{1,0:T(8,128)(2,1)S(1)}, u32[]{:S(2)}, u32[]{:S(2)}) collective-permute-start(bf16[128,1024]{1,0:T(8,128)(2,1)S(1)} %get-tuple-element.24), channel_id=1, source_target_pairs={{0,5},{1,4},{2,7},{3,6},{4,1},{5,0},{6,3},{7,2},{8,13},{9,12},{10,... | collective-permute-start | bytes 786440 | tf_op jit(solution)/shard_map/ppermute | solution.py:292
  68.8 3.8 %collective-permute-start.5 = (bf16[128,1024]{1,0:T(8,128)(2,1)S(1)}, bf16[128,1024]{1,0:T(8,128)(2,1)S(1)}, u32[]{:S(2)}, u32[]{:S(2)}) collective-permute-start(bf16[128,1024]{1,0:T(8,128)(2,1)S(1)} %get-tuple-element.25), channel_id=1, source_target_pairs={{0,7},{1,6},{2,5},{3,4},{4,3},{5,2},{6,1},{7,0},{8,15},{9,14},{10,... | collective-permute-start | bytes 786440 | tf_op jit(solution)/shard_map/ppermute | solution.py:292
  72.5 4.9 %far.3 = (bf16[128,1024]{1,0:T(8,128)(2,1)S(1)}, bf16[128,1024]{1,0:T(8,128)(2,1)S(1)}, bf16[128,1024]{1,0:T(8,128)(2,1)S(1)}, bf16[128,1024]{1,0:T(8,128)(2,1)S(1)}) custom-call(s32[184]{0:T(256)S(1)} %concatenate.3.refs_0_, bf16[1024,1024]{1,0:T(8,128)(2,1)S(1)} %bitcast.25, f32[6,144,1024]{2,1,0:T(8,128)S(1)} %get-tuple-element.18.refs_2_, ...), custom_call_target="tpu_custom_call" | custom-call | flops 2147483648 | bytes 6291456 | tf_op jit(solution)/shard_map/far/pallas_call | solution.py:250
  77.4 0.1 collective-permute-start.10
  77.5 0.3 collective-permute-start.6
  77.8 2.8 %collective-permute-start.8 = (bf16[128,1024]{1,0:T(8,128)(2,1)S(1)}, bf16[128,1024]{1,0:T(8,128)(2,1)S(1)}, u32[]{:S(2)}, u32[]{:S(2)}) collective-permute-start(bf16[128,1024]{1,0:T(8,128)(2,1)S(1)} %get-tuple-element.22), channel_id=1, source_target_pairs={{0,3},{1,2},{2,1},{3,0},{4,7},{5,6},{6,5},{7,4},{8,11},{9,10},{10,... | collective-permute-start | bytes 786440 | tf_op jit(solution)/shard_map/ppermute | solution.py:292
  80.6 0.0 collective-permute-done.4.refs_5_
  80.6 0.3 collective-permute-start.9
  81.0 1.6 %collective-permute-done.5.refs_7_ = bf16[128,1024]{1,0:T(8,128)(2,1)S(1)} collective-permute-done((bf16[128,1024]{1,0:T(8,128)(2,1)S(1)}, bf16[128,1024]{1,0:T(8,128)(2,1)S(1)}, u32[]{:S(2)}, u32[]{:S(2)}) %collective-permute-start.5) | collective-permute-done | bytes 262176 | tf_op jit(solution)/shard_map/ppermute | solution.py:292
  82.5 7.9 %near.3 = (f32[2,144,1024]{2,1,0:T(8,128)S(1)}, f32[2,8,1024]{2,1,0:T(8,128)S(1)}) custom-call(s32[184]{0:T(256)S(1)} %concatenate.3.refs_0_, bf16[1024,1024]{1,0:T(8,128)(2,1)S(1)} %bitcast.26, bf16[8,256,128]{2,1,0:T(8,128)(2,1)S(1)} %all-to-all-done.1.refs_2_.refs_4_, bf16[8,256,128]{2,1,0:T(8,128)(2,1)S(1)} %collective-permute-done.refs_3_.refs_5_, ...), custom_call_target="tpu_custom_call" | custom-call | flops 3221225472 | bytes 6291456 | tf_op jit(solution)/shard_map/near/pallas_call | solution.py:210
  90.4 4.2 %far.5 = (bf16[128,1024]{1,0:T(8,128)(2,1)S(1)}, bf16[128,1024]{1,0:T(8,128)(2,1)S(1)}) custom-call(s32[184]{0:T(256)S(1)} %concatenate.3.refs_0_, bf16[1024,1024]{1,0:T(8,128)(2,1)S(1)} %bitcast.27, f32[2,144,1024]{2,1,0:T(8,128)S(1)} %get-tuple-element.27.refs_2_, f32[2,8,1024]{2,1,0:T(8,128)S(1)} %get-tuple-element.28.refs_3_, ...), custom_call_target="tpu_custom_call" | custom-call | flops 1073741824 | bytes 6291456 | tf_op jit(solution)/shard_map/far/pallas_call | solution.py:250
  94.7 2.4 %collective-permute-start.7 = (bf16[128,1024]{1,0:T(8,128)(2,1)S(1)}, bf16[128,1024]{1,0:T(8,128)(2,1)S(1)}, u32[]{:S(2)}, u32[]{:S(2)}) collective-permute-start(bf16[128,1024]{1,0:T(8,128)(2,1)S(1)} %get-tuple-element.30), channel_id=1, source_target_pairs={{0,2},{1,3},{2,0},{3,1},{4,6},{5,7},{6,4},{7,5},{8,10},{9,11},{10,... | collective-permute-start | bytes 786440 | tf_op jit(solution)/shard_map/ppermute | solution.py:292
  97.1 0.0 collective-permute-done.10.refs_6_
  97.1 0.0 collective-permute-done.6.refs_1_
  97.1 0.0 collective-permute-done.8.refs_3_
  97.1 0.0 collective-permute-done.9.refs_4_
  97.1 1.1 %collective-permute-done.7.refs_2_ = bf16[128,1024]{1,0:T(8,128)(2,1)S(1)} collective-permute-done((bf16[128,1024]{1,0:T(8,128)(2,1)S(1)}, bf16[128,1024]{1,0:T(8,128)(2,1)S(1)}, u32[]{:S(2)}, u32[]{:S(2)}) %collective-permute-start.7) | collective-permute-done | bytes 262176 | tf_op jit(solution)/shard_map/ppermute | solution.py:292
  98.3 1.5 %unpack.1 = bf16[128,8192]{1,0:T(8,128)(2,1)} custom-call(s32[1]{0:T(128)} %bitcast.me_ref, bf16[128,1024]{1,0:T(8,128)(2,1)S(1)} %get-tuple-element.29.refs_0_, bf16[128,1024]{1,0:T(8,128)(2,1)S(1)} %collective-permute-done.6.refs_1_, bf16[128,1024]{1,0:T(8,128)(2,1)S(1)} %collective-permute-done.7.refs_2_, ...), custom_call_target="tpu_custom_call" | custom-call | tf_op jit(solution)/shard_map/unpack/pallas_call | solution.py:296
  (2 shorter events, 0.0 us)
Async XLA Ops:
  0.0 6.7 %copy-start = (bf16[128,8192]{1,0:T(8,128)(2,1)S(1)}, bf16[128,8192]{1,0:T(8,128)(2,1)}, u32[]{:S(2)}) copy-start(bf16[128,8192]{1,0:T(8,128)(2,1)} %param.4) | copy-start | bytes 6291460
  2.1 12.3 %all-to-all-start.1 = ((bf16[8,256,128]{2,1,0:T(8,128)(2,1)}), bf16[8,256,128]{2,1,0:T(8,128)(2,1)S(1)}, u32[]{:S(2)}, u32[]{:S(2)}) async-start(bf16[8,256,128]{2,1,0:T(8,128)(2,1)} %pack.1), calls=%async_computation.1 | async-start | bytes 1048576 | tf_op jit(solution)/shard_map/all_to_all | solution.py:325
  14.4 6.7 %copy-start.1 = (s32[32]{0:T(128)S(1)}, s32[32]{0:T(128)}, u32[]{:S(2)}) copy-start(s32[32]{0:T(128)} %param.7) | copy-start | bytes 388
  14.4 33.1 %all-to-all-start = ((bf16[8,128,1024]{2,1,0:T(8,128)(2,1)}), bf16[8,128,1024]{2,1,0:T(8,128)(2,1)S(1)}, u32[]{:S(2)}, u32[]{:S(2)}) async-start(bf16[8,128,1024]{2,1,0:T(8,128)(2,1)} %bitcast.28), calls=%async_computation | async-start | bytes 4194304 | tf_op jit(solution)/shard_map/all_to_all | solution.py:338
  19.6 13.1 %collective-permute-start = (bf16[8,256,128]{2,1,0:T(8,128)(2,1)S(1)}, bf16[8,256,128]{2,1,0:T(8,128)(2,1)S(1)}, u32[]{:S(2)}, u32[]{:S(2)}) collective-permute-start(bf16[8,256,128]{2,1,0:T(8,128)(2,1)S(1)} %all-to-all-done.1.refs_2_.refs_4_), channel_id=1, source_target_pairs={{0,8},{8,16},{16,24},{24,0},{1,9},{9,17},{17,25},{25,1},{2,10},{10... | collective-permute-start | bytes 1572872 | tf_op jit(solution)/shard_map/ppermute | solution.py:340
  20.9 24.7 %collective-permute-start.1 = (bf16[8,256,128]{2,1,0:T(8,128)(2,1)S(1)}, bf16[8,256,128]{2,1,0:T(8,128)(2,1)}, u32[]{:S(2)}, u32[]{:S(2)}) collective-permute-start(bf16[8,256,128]{2,1,0:T(8,128)(2,1)S(1)} %all-to-all-done.1.refs_2_.refs_4_), channel_id=1, source_target_pairs={{0,24},{8,0},{16,8},{24,16},{1,25},{9,1},{17,9},{25,17},{2,26},{10... | collective-permute-start | bytes 1572872 | tf_op jit(solution)/shard_map/ppermute | solution.py:341
  32.7 27.3 %collective-permute-start.2 = (bf16[8,256,128]{2,1,0:T(8,128)(2,1)S(1)}, bf16[8,256,128]{2,1,0:T(8,128)(2,1)}, u32[]{:S(2)}, u32[]{:S(2)}) collective-permute-start(bf16[8,256,128]{2,1,0:T(8,128)(2,1)S(1)} %collective-permute-done.refs_3_.refs_5_), channel_id=1, source_target_pairs={{8,16},{16,24},{9,17},{17,25},{10,18},{18,26},{11,19},{19,27},{12,... | collective-permute-start | bytes 1572872 | tf_op jit(solution)/shard_map/ppermute | solution.py:342
  45.6 14.4 %collective-permute-start.3 = (bf16[8,256,128]{2,1,0:T(8,128)(2,1)}, bf16[8,256,128]{2,1,0:T(8,128)(2,1)}, u32[]{:S(2)}, u32[]{:S(2)}) collective-permute-start(bf16[8,256,128]{2,1,0:T(8,128)(2,1)} %collective-permute-done.1.refs_4_.refs_6_), channel_id=1, source_target_pairs={{8,0},{16,8},{9,1},{17,9},{10,2},{18,10},{11,3},{19,11},{12,4},{20... | collective-permute-start | bytes 1572872 | tf_op jit(solution)/shard_map/ppermute | solution.py:343
  63.0 17.6 %collective-permute-start.4 = (bf16[128,1024]{1,0:T(8,128)(2,1)S(1)}, bf16[128,1024]{1,0:T(8,128)(2,1)S(1)}, u32[]{:S(2)}, u32[]{:S(2)}) collective-permute-start(bf16[128,1024]{1,0:T(8,128)(2,1)S(1)} %get-tuple-element.24), channel_id=1, source_target_pairs={{0,5},{1,4},{2,7},{3,6},{4,1},{5,0},{6,3},{7,2},{8,13},{9,12},{10,... | collective-permute-start | bytes 786440 | tf_op jit(solution)/shard_map/ppermute | solution.py:292
  68.8 13.8 %collective-permute-start.5 = (bf16[128,1024]{1,0:T(8,128)(2,1)S(1)}, bf16[128,1024]{1,0:T(8,128)(2,1)S(1)}, u32[]{:S(2)}, u32[]{:S(2)}) collective-permute-start(bf16[128,1024]{1,0:T(8,128)(2,1)S(1)} %get-tuple-element.25), channel_id=1, source_target_pairs={{0,7},{1,6},{2,5},{3,4},{4,3},{5,2},{6,1},{7,0},{8,15},{9,14},{10,... | collective-permute-start | bytes 786440 | tf_op jit(solution)/shard_map/ppermute | solution.py:292
  77.4 19.7 %collective-permute-start.10 = (bf16[128,1024]{1,0:T(8,128)(2,1)S(1)}, bf16[128,1024]{1,0:T(8,128)(2,1)S(1)}, u32[]{:S(2)}, u32[]{:S(2)}) collective-permute-start(bf16[128,1024]{1,0:T(8,128)(2,1)S(1)} %get-tuple-element.23), channel_id=1, source_target_pairs={{0,6},{1,7},{2,4},{3,5},{4,2},{5,3},{6,0},{7,1},{8,14},{9,15},{10,... | collective-permute-start | bytes 786440 | tf_op jit(solution)/shard_map/ppermute | solution.py:292
  77.5 19.6 %collective-permute-start.6 = (bf16[128,1024]{1,0:T(8,128)(2,1)S(1)}, bf16[128,1024]{1,0:T(8,128)(2,1)S(1)}, u32[]{:S(2)}, u32[]{:S(2)}) collective-permute-start(bf16[128,1024]{1,0:T(8,128)(2,1)S(1)} %get-tuple-element.20), channel_id=1, source_target_pairs={{0,1},{1,0},{2,3},{3,2},{4,5},{5,4},{6,7},{7,6},{8,9},{9,8},{10,11... | collective-permute-start | bytes 786440 | tf_op jit(solution)/shard_map/ppermute | solution.py:292
  77.8 19.3 %collective-permute-start.8 = (bf16[128,1024]{1,0:T(8,128)(2,1)S(1)}, bf16[128,1024]{1,0:T(8,128)(2,1)S(1)}, u32[]{:S(2)}, u32[]{:S(2)}) collective-permute-start(bf16[128,1024]{1,0:T(8,128)(2,1)S(1)} %get-tuple-element.22), channel_id=1, source_target_pairs={{0,3},{1,2},{2,1},{3,0},{4,7},{5,6},{6,5},{7,4},{8,11},{9,10},{10,... | collective-permute-start | bytes 786440 | tf_op jit(solution)/shard_map/ppermute | solution.py:292
  80.6 16.5 %collective-permute-start.9 = (bf16[128,1024]{1,0:T(8,128)(2,1)S(1)}, bf16[128,1024]{1,0:T(8,128)(2,1)S(1)}, u32[]{:S(2)}, u32[]{:S(2)}) collective-permute-start(bf16[128,1024]{1,0:T(8,128)(2,1)S(1)} %get-tuple-element.21), channel_id=1, source_target_pairs={{0,4},{1,5},{2,6},{3,7},{4,0},{5,1},{6,2},{7,3},{8,12},{9,13},{10,... | collective-permute-start | bytes 786440 | tf_op jit(solution)/shard_map/ppermute | solution.py:292
  94.7 3.6 %collective-permute-start.7 = (bf16[128,1024]{1,0:T(8,128)(2,1)S(1)}, bf16[128,1024]{1,0:T(8,128)(2,1)S(1)}, u32[]{:S(2)}, u32[]{:S(2)}) collective-permute-start(bf16[128,1024]{1,0:T(8,128)(2,1)S(1)} %get-tuple-element.30), channel_id=1, source_target_pairs={{0,2},{1,3},{2,0},{3,1},{4,6},{5,7},{6,4},{7,5},{8,10},{9,11},{10,... | collective-permute-start | bytes 786440 | tf_op jit(solution)/shard_map/ppermute | solution.py:292
